TPU v7x, 32 devices: a whole 2x2x4 slice. The times are simulated.
32 devices in a mesh: island: 4 (over z), fsdp: 4 (over y, core), tp: 2 (over x).
Axes of the slice: x: 2, y: 2, z: 4, core: 2. Of those that a mesh axis runs over, the one named last changes fastest.
Arguments:
- context: bfloat16 [4096, 3072], P(('island', 'fsdp'), 'tp'), may hold values from -6 to 6
- residual: bfloat16 [4096, 6144], P(('island', 'fsdp'), 'tp'), may hold values from -32 to 32
- cotangent: bfloat16 [4096, 6144], P(('island', 'fsdp'), 'tp'), may hold values from -8 to 8
- gain: bfloat16 [6144], replicated, may hold values from 0.5 to 1.5
- weight: bfloat16 [3072, 6144], P('tp', 'fsdp'), may hold values from -1 to 1
- first_moment: bfloat16 [4, 3072, 6144], P('island', 'tp', 'fsdp'), may hold values from -0.011962891 to 0.011962891
- second_moment: bfloat16 [4, 3072, 6144], P('island', 'tp', 'fsdp'), may hold values from 9.9651515e-08 to 9.983778e-07
- momentum: float32 [3072, 6144], P('tp', 'fsdp'), may hold values from -3 to 3
Outputs:
- new_momentum: float32 [3072, 6144], P('tp', 'fsdp')
- outer_step: bfloat16 [3072, 6144], P('tp', 'fsdp')
All inputs are finite; a program needn't handle non-finite values.
Results may differ from a plain program's by a relative error of at most 0.014.
Values may be sent and summed in bfloat16 or wider, within the bound.
No kernel may reach another device: no remote copies, remote signals or barrier semaphores. Data moves between devices by JAX's collectives and lax.ppermute only.
A program may use at most 192 MiB of HBM per device.

v0:
```python
import jax
import jax.numpy as jnp
from jax import lax
from jax.sharding import PartitionSpec as P

norm_eps = 1e-06
adam_eps = 1e-08
beta_one = 0.9
beta_two = 0.999
bias_one = 1.0 - 0.9**10
bias_two = 1.0 - 0.999**10
decay_rate = 0.1
outer_mu = 0.9

f32 = jnp.float32
bf16 = jnp.bfloat16


def outer_update(delta, momentum):
    new_momentum = outer_mu * momentum + delta
    outer_step = (delta + outer_mu * new_momentum).astype(bf16)
    return (new_momentum, outer_step)


def swap(value, axis, bit):
    count = lax.axis_size(axis)
    return lax.ppermute(value, axis, [(i, i ^ bit) for i in range(count)])


def tie(value, *others):
    return lax.optimization_barrier((value,) + others)[0]


class IslandLine:
    def __init__(self, total_chunks):
        self.n = lax.axis_size("island")
        self.me = lax.axis_index("island")
        self.chunks = total_chunks
        self.parts = []
        self.sent = ([], [])
        self.came = ([], [])

    def pick(self, choices):
        items = sorted(choices.items())
        value = items[-1][1]
        for at, other in reversed(items[:-1]):
            value = jnp.where(self.me == at, other, value)
        return value

    def stage(self):
        s = len(self.sent[0])
        n, half = self.n, self.n // 2
        used = [k for k in range(s - half + 1, s + 1) if 0 <= k < self.chunks]
        last = [] if s == 0 else [self.came[0][-1], self.came[1][-1], self.sent[0][-1], self.sent[1][-1]]
        held = lax.optimization_barrier(tuple(last + [self.parts[k] for k in used]))
        came, sent = held[:2], held[2:4]
        parts = dict(zip(used, held[len(last) :]))
        fresh = []
        for way in (0, 1):
            choices = {}
            for i in range(n - 1):
                at = i if way == 0 else n - 1 - i
                k = s - i
                if not 0 <= k < self.chunks:
                    continue
                if i == 0:
                    value = parts[k]
                elif i < half:
                    value = (came[way].astype(f32) + parts[k].astype(f32)).astype(bf16)
                elif i == half:
                    value = (came[way].astype(f32) + sent[1 - way].astype(f32)).astype(bf16)
                else:
                    value = came[way]
                choices[at] = value
            fresh.append((self.pick(choices), sorted(choices)))
        for way in (0, 1):
            value, sources = fresh[way]
            move = 1 if way == 0 else -1
            self.sent[way].append(value)
            self.came[way].append(lax.ppermute(value, "island", [(i, i + move) for i in sources]))

    def add(self, part):
        self.parts.append(part)
        self.stage()

    def total(self, k):
        n, half = self.n, self.n // 2
        choices = {0: self.came[1][k + n - 2], n - 1: self.came[0][k + n - 2]}
        for i in range(1, n - 1):
            choices[i] = self.sent[1][k + n - 1 - i] if i < half else self.sent[0][k + i]
        spots = sorted(choices)
        return self.pick(dict(zip(spots, lax.optimization_barrier(tuple(choices[i] for i in spots)))))


def body(context, residual, cotangent, gain, weight, first_moment, second_moment, momentum):
    tok_rows = context.shape[0]
    width = gain.shape[0]
    fsdp_count = lax.axis_size("fsdp")
    group = fsdp_count // 2
    cols = weight.shape[1]
    t = lax.axis_index("tp")
    f = lax.axis_index("fsdp")
    high = f // group
    low = f % group
    near = t == high

    pieces = 2
    rows = tok_rows // pieces

    def regroup(array):
        parts = []
        for r in range(group):
            part = lax.dynamic_slice_in_dim(array, (low ^ r) * cols, cols, axis=1)
            parts.append(swap(part, "fsdp", r) if r else part)
        return parts

    def project(block):
        return lax.optimization_barrier(
            jnp.dot(block, weight, preferred_element_type=f32).astype(bf16)
        )

    far_pieces = [[swap(context[p * rows : (p + 1) * rows], "fsdp", group) for p in range(pieces)]]
    near_blocks = [context] + [swap(context, "fsdp", r) for r in range(1, group)]
    for r in range(1, group):
        far_pieces.append([swap(piece, "fsdp", r) for piece in far_pieces[0]])
    near_out = [project(context)]
    issued = near_out[0]
    far_outs = []
    for r in range(group):
        for p in range(pieces):
            issued = project(tie(far_pieces[r][p], issued))
            far_outs.append(swap(issued, "fsdp", group))
        if r + 1 < group:
            near_out.append(project(tie(near_blocks[r + 1], issued)))
            issued = tie(issued, near_out[-1])

    residual_parts = regroup(residual)
    cotangent_parts = regroup(cotangent)
    gain_part = lax.dynamic_slice_in_dim(gain, t * (width // 2) + low * cols, cols).astype(f32)

    hidden, weighted, sums = [], [], []
    for r in range(group):
        for p in range(pieces):
            span = slice(p * rows, (p + 1) * rows)
            far_out, own_out, _ = lax.optimization_barrier(
                (far_outs[r * pieces + p], near_out[r], issued)
            )
            own_out = own_out[span]
            keep = jnp.where(near, own_out, far_out)
            came = swap(jnp.where(near, far_out, own_out), "tp", 1)
            keep, came, res, cot = lax.optimization_barrier(
                (keep, came, residual_parts[r], cotangent_parts[r])
            )
            h = res[span].astype(f32) + keep.astype(f32) + came.astype(f32)
            w = gain_part[None, :] * cot[span].astype(f32)
            hidden.append(h)
            weighted.append(w)
            sums.append(jnp.stack([jnp.sum(h * h, axis=-1), jnp.sum(h * w, axis=-1)]))
    own_sums = jnp.concatenate(sums, axis=1)
    totals = own_sums
    for r in range(1, group):
        came = swap(own_sums, "fsdp", r)
        order = [r ^ k for k in range(group)]
        came = jnp.concatenate(
            [came[:, k * tok_rows : (k + 1) * tok_rows] for k in order], axis=1
        )
        totals = totals + came
    totals = totals + swap(totals, "tp", 1)
    inv_rms = lax.rsqrt(totals[0] / width + norm_eps)
    pull = inv_rms**3 * totals[1] / width

    tokens = near_blocks + [piece for block in far_pieces for piece in block]
    context_all = jnp.concatenate(tokens, axis=0)
    narrow = 128
    units = cols // narrow
    widths = [1, 1, 2]
    while sum(widths) < units:
        widths.append(min(4, units - sum(widths)))
    unit_rows = weight.shape[0]
    chunk_rows = 1024 if units * unit_rows % 1024 == 0 else unit_rows
    chunk_count = units * unit_rows // chunk_rows
    streams = 2
    lines = [IslandLine(len(range(k, chunk_count, streams))) for k in range(streams)]

    def stretch(items, size, lo, hi):
        found = []
        for k in range(lo // size, -(-hi // size)):
            first, last = max(lo - k * size, 0), min(hi - k * size, size)
            found.append(items[k][first:last])
        return found[0] if len(found) == 1 else jnp.concatenate(found, axis=0)

    parts = []
    added = 0
    pseudos, arrivals = [], []
    k = 0
    for c, wide in enumerate(widths):
        cols_at = slice(k * narrow, (k + wide) * narrow)
        d_local = jnp.concatenate(
            [
                weighted[j][:, cols_at] * inv_rms[j * rows : (j + 1) * rows, None]
                - hidden[j][:, cols_at] * pull[j * rows : (j + 1) * rows, None]
                for j in range(group * pieces)
            ],
            axis=0,
        ).astype(bf16)
        if c in (2, 3):
            d_local = tie(d_local, arrivals[c - 2 if c == 2 else 2])
        elif c > 3:
            d_local = tie(d_local, pseudos[c - 2])
        came = swap(d_local, "tp", 1)
        if c:
            came = tie(came, d_sent)
        arrivals.append(came)
        d_own = jnp.where(near, d_local, came)
        d_sent = jnp.where(near, came, d_local)
        d_far = swap(d_sent, "fsdp", group)
        d_all = jnp.concatenate([d_own, d_far], axis=0)
        grad = lax.dot_general(
            context_all, d_all, (((0,), (0,)), ((), ())), preferred_element_type=f32
        ) / (tok_rows * fsdp_count)
        first = first_moment[0, :, cols_at].astype(f32)
        second = second_moment[0, :, cols_at].astype(f32)
        m_new = beta_one * first + (1.0 - beta_one) * grad
        v_new = beta_two * second + (1.0 - beta_two) * grad * grad
        update = m_new / bias_one / (
            jnp.sqrt(v_new / bias_two) + adam_eps
        ) + decay_rate * weight[:, cols_at].astype(f32)
        pseudos.append(lax.optimization_barrier(update.astype(bf16)))
        parts += [pseudos[c][:, u * narrow : (u + 1) * narrow] for u in range(wide)]
        k += wide
        while (added + 1) * chunk_rows <= len(parts) * unit_rows:
            part = stretch(parts, unit_rows, added * chunk_rows, (added + 1) * chunk_rows)
            lines[added % streams].add(part)
            added += 1
    for line in lines * (lines[0].n - 2):
        line.stage()
    totals = [lines[k % streams].total(k // streams) for k in range(chunk_count)]
    momentum_out, step_out = [], []
    for k in range(units):
        cols_at = slice(k * narrow, (k + 1) * narrow)
        total = stretch(totals, chunk_rows, k * unit_rows, (k + 1) * unit_rows)
        delta = total.astype(f32) / lax.axis_size("island")
        new_momentum, outer_step = outer_update(delta, momentum[:, cols_at])
        momentum_out.append(new_momentum)
        step_out.append(outer_step)
    return (jnp.concatenate(momentum_out, axis=1), jnp.concatenate(step_out, axis=1))


def solution(mesh):
    in_specs = (
        P(("island", "fsdp"), "tp"),
        P(("island", "fsdp"), "tp"),
        P(("island", "fsdp"), "tp"),
        P(),
        P("tp", "fsdp"),
        P("island", "tp", "fsdp"),
        P("island", "tp", "fsdp"),
        P("tp", "fsdp"),
    )
    out_specs = (P("tp", "fsdp"), P("tp", "fsdp"))
    return jax.shard_map(body, mesh=mesh, in_specs=in_specs, out_specs=out_specs, check_vma=False)
```

profile of v0, /device:TPU:2, one launch (start us, length us, event | category | flops | bytes accessed | tf_op | source)
XLA Modules:
  0.0 292.9 jit_solution(3794696547832866245)
XLA Ops:
  0.7 2.2 fusion.288
  4.9 2.4 constant_dynamic-slice_fusion.3
  7.3 4.6 %convolution_convert_fusion.1 = bf16[256,1536]{1,0:T(8,128)(2,1)} fusion(bf16[256,1536]{1,0:T(8,128)(2,1)S(1)} %copy-done, bf16[1536,1536]{1,0:T(8,128)(2,1)} %param.12), kind=kOutput, calls=%fused_computation.19 | convolution fusion | flops 1208352768 | bytes 6291456 | tf_op jit(solution)/shard_map/dot_general | solution.py:119
  12.8 2.4 constant_dynamic-slice_fusion.2
  16.0 7.1 %collective-permute-done.1 = bf16[128,1536]{1,0:T(8,128)(2,1)} collective-permute-done((bf16[128,1536]{1,0:T(8,128)(2,1)}, bf16[128,1536]{1,0:T(8,128)(2,1)}, u32[]{:S(2)}, u32[]{:S(2)}) %collective-permute-start.1) | collective-permute-done | bytes 393248 | tf_op jit(solution)/shard_map/ppermute | solution.py:27
  23.1 3.3 %convolution_convert_fusion.5 = bf16[128,1536]{1,0:T(8,128)(2,1)S(1)} fusion(bf16[128,1536]{1,0:T(8,128)(2,1)} %collective-permute-done.1, bf16[1536,1536]{1,0:T(8,128)(2,1)} %param.12), kind=kOutput, calls=%fused_computation.23 | convolution fusion | flops 604176384 | bytes 5505024 | tf_op jit(solution)/shard_map/dot_general | solution.py:119
  28.2 3.1 %convolution_convert_fusion.2 = bf16[128,1536]{1,0:T(8,128)(2,1)S(1)} fusion(bf16[128,1536]{1,0:T(8,128)(2,1)S(1)} %collective-permute-done.2, bf16[1536,1536]{1,0:T(8,128)(2,1)} %param.12), kind=kOutput, calls=%fused_computation.20 | convolution fusion | flops 604176384 | bytes 5505024 | tf_op jit(solution)/shard_map/dot_general | solution.py:119
  33.6 12.8 %collective-permute-done.7 = bf16[128,1536]{1,0:T(8,128)(2,1)S(1)} collective-permute-done((bf16[128,1536]{1,0:T(8,128)(2,1)S(1)}, bf16[128,1536]{1,0:T(8,128)(2,1)S(1)}, u32[]{:S(2)}, u32[]{:S(2)}) %collective-permute-start.7) | collective-permute-done | bytes 393248 | tf_op jit(solution)/shard_map/ppermute | solution.py:27
  48.9 2.7 convolution_convert_fusion
  53.9 4.5 %collective-permute-done.13 = bf16[128,1536]{1,0:T(8,128)(2,1)S(1)} collective-permute-done((bf16[128,1536]{1,0:T(8,128)(2,1)S(1)}, bf16[128,1536]{1,0:T(8,128)(2,1)S(1)}, u32[]{:S(2)}, u32[]{:S(2)}) %collective-permute-start.13) | collective-permute-done | bytes 393248 | tf_op jit(solution)/shard_map/ppermute | solution.py:27
  58.7 6.8 %collective-permute-done.9 = bf16[128,1536]{1,0:T(8,128)(2,1)S(1)} collective-permute-done((bf16[128,1536]{1,0:T(8,128)(2,1)S(1)}, bf16[128,1536]{1,0:T(8,128)(2,1)S(1)}, u32[]{:S(2)}, u32[]{:S(2)}) %collective-permute-start.9) | collective-permute-done | bytes 393248 | tf_op jit(solution)/shard_map/ppermute | solution.py:27
  68.2 15.8 %collective-permute-done.14 = bf16[128,1536]{1,0:T(8,128)(2,1)S(1)} collective-permute-done((bf16[128,1536]{1,0:T(8,128)(2,1)S(1)}, bf16[128,1536]{1,0:T(8,128)(2,1)S(1)}, u32[]{:S(2)}, u32[]{:S(2)}) %collective-permute-start.14) | collective-permute-done | bytes 393248 | tf_op jit(solution)/shard_map/ppermute | solution.py:27
  84.0 2.1 multiply_reduce_fusion.7
  87.8 3.2 %collective-permute-done.16 = f32[2,512]{1,0:T(2,128)S(1)} collective-permute-done((f32[2,512]{1,0:T(2,128)S(1)}, f32[2,512]{1,0:T(2,128)S(1)}, u32[]{:S(2)}, u32[]{:S(2)}) %collective-permute-start.16) | collective-permute-done | bytes 4128 | tf_op jit(solution)/shard_map/ppermute | solution.py:27
  92.5 1.7 collective-permute-start.17
  94.3 5.0 %collective-permute-done.17 = bf16[512,128]{1,0:T(8,128)(2,1)S(1)} collective-permute-done((bf16[512,128]{1,0:T(8,128)(2,1)S(1)}, bf16[512,128]{1,0:T(8,128)(2,1)S(1)}, u32[]{:S(2)}, u32[]{:S(2)}) %collective-permute-start.17) | collective-permute-done | bytes 131104 | tf_op jit(solution)/shard_map/ppermute | solution.py:27
  102.0 2.4 collective-permute-done.18
  104.4 2.6 fusion.57
  107.7 3.7 %collective-permute-start.19 = (bf16[1024,128]{1,0:T(8,128)(2,1)S(1)}, bf16[1024,128]{1,0:T(8,128)(2,1)S(1)}, u32[]{:S(2)}, u32[]{:S(2)}) collective-permute-start(bf16[1024,128]{1,0:T(8,128)(2,1)S(1)} %slice.610), channel_id=1, source_target_pairs={{0,8},{1,9},{2,10},{3,11},{4,12},{5,13},{6,14},{7,15}} | collective-permute-start | bytes 786440 | tf_op jit(solution)/shard_map/ppermute | solution.py:80
  111.4 2.6 fusion.58
  119.1 3.4 %collective-permute-done.26 = bf16[512,256]{1,0:T(8,128)(2,1)S(1)} collective-permute-done((bf16[512,256]{1,0:T(8,128)(2,1)S(1)}, bf16[512,256]{1,0:T(8,128)(2,1)S(1)}, u32[]{:S(2)}, u32[]{:S(2)}) %collective-permute-start.26) | collective-permute-done | bytes 262176 | tf_op jit(solution)/shard_map/ppermute | solution.py:27
  123.9 3.7 %fusion.20 = bf16[1536,256]{1,0:T(8,128)(2,1)S(1)} fusion(bf16[1536,1536]{1,0:T(8,128)(2,1)S(1)} %bitcast.146, bf16[1,1536,1536]{2,1,0:T(8,128)(2,1)} %param.14, bf16[1,1536,1536]{2,1,0:T(8,128)(2,1)} %param.13, bf16[1024,1536]{1,0:T(8,128)(2,1)S(1)} %constant_dynamic-update-slice_fusion, bf16[512,256]{1,0:T(8,128)(2,1)S(1)} %collective-permute-done.26, ...), kind=kOutput, calls=%fused_computation.32 | convolution fusion | flops 813432832 | bytes 6815744 | tf_op jit(solution)/shard_map/dot_general | solution.py:218
  128.6 4.3 %collective-permute-start.31 = (bf16[1024,128]{1,0:T(8,128)(2,1)S(1)}, bf16[1024,128]{1,0:T(8,128)(2,1)S(1)}, u32[]{:S(2)}, u32[]{:S(2)}) collective-permute-start(bf16[1024,128]{1,0:T(8,128)(2,1)S(1)} %get-tuple-element.269), channel_id=1, source_target_pairs={{0,8},{8,16},{1,9},{9,17},{2,10},{10,18},{3,11},{11,19},{4,12},{12... | collective-permute-start | bytes 786440 | tf_op jit(solution)/shard_map/ppermute | solution.py:80
  134.2 4.6 %collective-permute-start.28 = (bf16[1024,128]{1,0:T(8,128)(2,1)S(1)}, bf16[1024,128]{1,0:T(8,128)(2,1)S(1)}, u32[]{:S(2)}, u32[]{:S(2)}) collective-permute-start(bf16[1024,128]{1,0:T(8,128)(2,1)S(1)} %get-tuple-element.281), channel_id=1, source_target_pairs={{0,8},{8,16},{16,24},{1,9},{9,17},{17,25},{2,10},{10,18},{18,26},{... | collective-permute-start | bytes 786440 | tf_op jit(solution)/shard_map/ppermute | solution.py:80
  140.4 4.6 %collective-permute-start.34 = (bf16[1024,128]{1,0:T(8,128)(2,1)S(1)}, bf16[1024,128]{1,0:T(8,128)(2,1)S(1)}, u32[]{:S(2)}, u32[]{:S(2)}) collective-permute-start(bf16[1024,128]{1,0:T(8,128)(2,1)S(1)} %get-tuple-element.291), channel_id=1, source_target_pairs={{0,8},{8,16},{16,24},{1,9},{9,17},{17,25},{2,10},{10,18},{18,26},{... | collective-permute-start | bytes 786440 | tf_op jit(solution)/shard_map/ppermute | solution.py:80
  148.8 4.4 %collective-permute-done.33 = bf16[1024,128]{1,0:T(8,128)(2,1)S(1)} collective-permute-done((bf16[1024,128]{1,0:T(8,128)(2,1)S(1)}, bf16[1024,128]{1,0:T(8,128)(2,1)S(1)}, u32[]{:S(2)}, u32[]{:S(2)}) %collective-permute-start.33) | collective-permute-done | bytes 262176 | tf_op jit(solution)/shard_map/ppermute | solution.py:80
  156.0 3.7 %collective-permute-done.36 = bf16[512,512]{1,0:T(8,128)(2,1)S(1)} collective-permute-done((bf16[512,512]{1,0:T(8,128)(2,1)S(1)}, bf16[512,512]{1,0:T(8,128)(2,1)S(1)}, u32[]{:S(2)}, u32[]{:S(2)}) %collective-permute-start.36) | collective-permute-done | bytes 524320 | tf_op jit(solution)/shard_map/ppermute | solution.py:27
  159.8 5.8 %fusion.12 = bf16[1536,512]{1,0:T(8,128)(2,1)S(1)} fusion(bf16[1536,1536]{1,0:T(8,128)(2,1)S(1)} %bitcast.146, bf16[1,1536,1536]{2,1,0:T(8,128)(2,1)} %param.14, bf16[1,1536,1536]{2,1,0:T(8,128)(2,1)} %param.13, bf16[1024,1536]{1,0:T(8,128)(2,1)S(1)} %constant_dynamic-update-slice_fusion, bf16[512,512]{1,0:T(8,128)(2,1)S(1)} %collective-permute-done.36, ...), kind=kOutput, calls=%fused_computation.16 | convolution fusion | flops 1626865664 | bytes 10485760 | tf_op jit(solution)/shard_map/dot_general | solution.py:218
  166.2 5.3 %collective-permute-start.40 = (bf16[1024,128]{1,0:T(8,128)(2,1)S(1)}, bf16[1024,128]{1,0:T(8,128)(2,1)S(1)}, u32[]{:S(2)}, u32[]{:S(2)}) collective-permute-start(bf16[1024,128]{1,0:T(8,128)(2,1)S(1)} %get-tuple-element.311), channel_id=1, source_target_pairs={{0,8},{8,16},{16,24},{1,9},{9,17},{17,25},{2,10},{10,18},{18,26},{... | collective-permute-start | bytes 786440 | tf_op jit(solution)/shard_map/ppermute | solution.py:80
  173.1 4.6 %collective-permute-start.38 = (bf16[1024,128]{1,0:T(8,128)(2,1)S(1)}, bf16[1024,128]{1,0:T(8,128)(2,1)S(1)}, u32[]{:S(2)}, u32[]{:S(2)}) collective-permute-start(bf16[1024,128]{1,0:T(8,128)(2,1)S(1)} %get-tuple-element.301), channel_id=1, source_target_pairs={{0,8},{8,16},{16,24},{1,9},{9,17},{17,25},{2,10},{10,18},{18,26},{... | collective-permute-start | bytes 786440 | tf_op jit(solution)/shard_map/ppermute | solution.py:80
  180.3 3.5 %collective-permute-start.44 = (bf16[1024,128]{1,0:T(8,128)(2,1)S(1)}, bf16[1024,128]{1,0:T(8,128)(2,1)S(1)}, u32[]{:S(2)}, u32[]{:S(2)}) collective-permute-start(bf16[1024,128]{1,0:T(8,128)(2,1)S(1)} %get-tuple-element.331), channel_id=1, source_target_pairs={{0,8},{8,16},{16,24},{1,9},{9,17},{17,25},{2,10},{10,18},{18,26},{... | collective-permute-start | bytes 786440 | tf_op jit(solution)/shard_map/ppermute | solution.py:80
  185.4 5.8 %fusion.13 = bf16[1536,512]{1,0:T(8,128)(2,1)S(1)} fusion(bf16[1536,1536]{1,0:T(8,128)(2,1)S(1)} %bitcast.146, bf16[1,1536,1536]{2,1,0:T(8,128)(2,1)} %param.14, bf16[1,1536,1536]{2,1,0:T(8,128)(2,1)} %param.13, bf16[1024,1536]{1,0:T(8,128)(2,1)S(1)} %constant_dynamic-update-slice_fusion, bf16[512,512]{1,0:T(8,128)(2,1)S(1)} %collective-permute-done.50, ...), kind=kOutput, calls=%fused_computation.17 | convolution fusion | flops 1626865664 | bytes 10485760 | tf_op jit(solution)/shard_map/dot_general | solution.py:218
  191.7 4.6 %collective-permute-start.42 = (bf16[1024,128]{1,0:T(8,128)(2,1)S(1)}, bf16[1024,128]{1,0:T(8,128)(2,1)S(1)}, u32[]{:S(2)}, u32[]{:S(2)}) collective-permute-start(bf16[1024,128]{1,0:T(8,128)(2,1)S(1)} %get-tuple-element.321), channel_id=1, source_target_pairs={{0,8},{8,16},{16,24},{1,9},{9,17},{17,25},{2,10},{10,18},{18,26},{... | collective-permute-start | bytes 786440 | tf_op jit(solution)/shard_map/ppermute | solution.py:80
  199.1 4.6 %collective-permute-start.48 = (bf16[1024,128]{1,0:T(8,128)(2,1)S(1)}, bf16[1024,128]{1,0:T(8,128)(2,1)S(1)}, u32[]{:S(2)}, u32[]{:S(2)}) collective-permute-start(bf16[1024,128]{1,0:T(8,128)(2,1)S(1)} %get-tuple-element.353), channel_id=1, source_target_pairs={{0,8},{8,16},{16,24},{1,9},{9,17},{17,25},{2,10},{10,18},{18,26},{... | collective-permute-start | bytes 786440 | tf_op jit(solution)/shard_map/ppermute | solution.py:80
  205.4 4.6 %collective-permute-start.46 = (bf16[1024,128]{1,0:T(8,128)(2,1)S(1)}, bf16[1024,128]{1,0:T(8,128)(2,1)S(1)}, u32[]{:S(2)}, u32[]{:S(2)}) collective-permute-start(bf16[1024,128]{1,0:T(8,128)(2,1)S(1)} %get-tuple-element.343), channel_id=1, source_target_pairs={{0,8},{8,16},{16,24},{1,9},{9,17},{17,25},{2,10},{10,18},{18,26},{... | collective-permute-start | bytes 786440 | tf_op jit(solution)/shard_map/ppermute | solution.py:80
  214.2 2.1 collective-permute-done.46
  216.3 4.7 %collective-permute-done.45 = bf16[1024,128]{1,0:T(8,128)(2,1)S(1)} collective-permute-done((bf16[1024,128]{1,0:T(8,128)(2,1)S(1)}, bf16[1024,128]{1,0:T(8,128)(2,1)S(1)}, u32[]{:S(2)}, u32[]{:S(2)}) %collective-permute-start.45) | collective-permute-done | bytes 262176 | tf_op jit(solution)/shard_map/ppermute | solution.py:80
  221.3 2.0 collective-permute-start.54
  224.9 4.6 %collective-permute-start.52 = (bf16[1024,128]{1,0:T(8,128)(2,1)S(1)}, bf16[1024,128]{1,0:T(8,128)(2,1)S(1)}, u32[]{:S(2)}, u32[]{:S(2)}) collective-permute-start(bf16[1024,128]{1,0:T(8,128)(2,1)S(1)} %get-tuple-element.363), channel_id=1, source_target_pairs={{0,8},{8,16},{16,24},{1,9},{9,17},{17,25},{2,10},{10,18},{18,26},{... | collective-permute-start | bytes 786440 | tf_op jit(solution)/shard_map/ppermute | solution.py:80
  233.7 3.1 %collective-permute-start.58 = (bf16[1024,128]{1,0:T(8,128)(2,1)S(1)}, bf16[1024,128]{1,0:T(8,128)(2,1)S(1)}, u32[]{:S(2)}, u32[]{:S(2)}) collective-permute-start(bf16[1024,128]{1,0:T(8,128)(2,1)S(1)} %get-tuple-element.393), channel_id=1, source_target_pairs={{0,8},{8,16},{16,24},{1,9},{9,17},{17,25},{2,10},{10,18},{18,26},{... | collective-permute-start | bytes 786440 | tf_op jit(solution)/shard_map/ppermute | solution.py:80
  238.1 2.1 collective-permute-done.51
  240.5 2.5 collective-permute-start.56
  246.2 4.1 %collective-permute-start.62 = (bf16[1024,128]{1,0:T(8,128)(2,1)S(1)}, bf16[1024,128]{1,0:T(8,128)(2,1)S(1)}, u32[]{:S(2)}, u32[]{:S(2)}) collective-permute-start(bf16[1024,128]{1,0:T(8,128)(2,1)S(1)} %get-tuple-element.412), channel_id=1, source_target_pairs={{0,8},{8,16},{16,24},{1,9},{9,17},{17,25},{2,10},{10,18},{18,26},{... | collective-permute-start | bytes 786440 | tf_op jit(solution)/shard_map/ppermute | solution.py:80
  252.6 4.0 %collective-permute-start.60 = (bf16[1024,128]{1,0:T(8,128)(2,1)S(1)}, bf16[1024,128]{1,0:T(8,128)(2,1)S(1)}, u32[]{:S(2)}, u32[]{:S(2)}) collective-permute-start(bf16[1024,128]{1,0:T(8,128)(2,1)S(1)} %get-tuple-element.403), channel_id=1, source_target_pairs={{0,8},{8,16},{16,24},{1,9},{9,17},{17,25},{2,10},{10,18},{18,26},{... | collective-permute-start | bytes 786440 | tf_op jit(solution)/shard_map/ppermute | solution.py:80
  263.0 4.1 %collective-permute-done.59 = bf16[1024,128]{1,0:T(8,128)(2,1)S(1)} collective-permute-done((bf16[1024,128]{1,0:T(8,128)(2,1)S(1)}, bf16[1024,128]{1,0:T(8,128)(2,1)S(1)}, u32[]{:S(2)}, u32[]{:S(2)}) %collective-permute-start.59) | collective-permute-done | bytes 262176 | tf_op jit(solution)/shard_map/ppermute | solution.py:80
  273.7 4.1 %collective-permute-done.63 = bf16[1024,128]{1,0:T(8,128)(2,1)S(1)} collective-permute-done((bf16[1024,128]{1,0:T(8,128)(2,1)S(1)}, bf16[1024,128]{1,0:T(8,128)(2,1)S(1)}, u32[]{:S(2)}, u32[]{:S(2)}) %collective-permute-start.63) | collective-permute-done | bytes 262176 | tf_op jit(solution)/shard_map/ppermute | solution.py:80
  281.1 5.8 %collective-permute-done.67 = bf16[1024,128]{1,0:T(8,128)(2,1)S(1)} collective-permute-done((bf16[1024,128]{1,0:T(8,128)(2,1)S(1)}, bf16[1024,128]{1,0:T(8,128)(2,1)S(1)}, u32[]{:S(2)}, u32[]{:S(2)}) %collective-permute-start.67) | collective-permute-done | bytes 262176 | tf_op jit(solution)/shard_map/ppermute | solution.py:80
  289.2 3.7 %copy-done.4 = f32[1536,1536]{1,0:T(8,128)} copy-done((f32[1536,1536]{1,0:T(8,128)}, f32[1536,1536]{1,0:T(8,128)S(1)}, u32[]{:S(2)}) %copy-start.4) | copy-done | bytes 9437208
  (253 shorter events, 85.8 us)
Async XLA Ops:
  0.6 47.8 %collective-permute-start = (bf16[256,1536]{1,0:T(8,128)(2,1)}, bf16[256,1536]{1,0:T(8,128)(2,1)}, u32[]{:S(2)}, u32[]{:S(2)}) collective-permute-start(bf16[256,1536]{1,0:T(8,128)(2,1)} %param.8), channel_id=1, source_target_pairs={{0,2},{2,0},{4,6},{6,4},{1,3},{3,1},{5,7},{7,5},{8,10},{10,8},{12,... | collective-permute-start | bytes 2359304 | tf_op jit(solution)/shard_map/ppermute | solution.py:27
  2.9 25.1 %collective-permute-start.2 = (bf16[128,1536]{1,0:T(8,128)(2,1)}, bf16[128,1536]{1,0:T(8,128)(2,1)S(1)}, u32[]{:S(2)}, u32[]{:S(2)}) collective-permute-start(bf16[128,1536]{1,0:T(8,128)(2,1)} %get-tuple-element.504), channel_id=1, source_target_pairs={{0,4},{2,6},{4,0},{6,2},{1,5},{3,7},{5,1},{7,3},{8,12},{10,14},{12... | collective-permute-start | bytes 1179656 | tf_op jit(solution)/shard_map/ppermute | solution.py:27
  4.4 18.7 %collective-permute-start.1 = (bf16[128,1536]{1,0:T(8,128)(2,1)}, bf16[128,1536]{1,0:T(8,128)(2,1)}, u32[]{:S(2)}, u32[]{:S(2)}) collective-permute-start(bf16[128,1536]{1,0:T(8,128)(2,1)} %get-tuple-element.505), channel_id=1, source_target_pairs={{0,4},{2,6},{4,0},{6,2},{1,5},{3,7},{5,1},{7,3},{8,12},{10,14},{12... | collective-permute-start | bytes 1179656 | tf_op jit(solution)/shard_map/ppermute | solution.py:27
  7.3 61.0 %collective-permute-start.11 = (bf16[256,1536]{1,0:T(8,128)(2,1)}, bf16[256,1536]{1,0:T(8,128)(2,1)}, u32[]{:S(2)}, u32[]{:S(2)}) collective-permute-start(bf16[256,1536]{1,0:T(8,128)(2,1)} %get-tuple-element.483), channel_id=1, source_target_pairs={{0,2},{2,0},{4,6},{6,4},{1,3},{3,1},{5,7},{7,5},{8,10},{10,8},{12,... | collective-permute-start | bytes 2359304 | tf_op jit(solution)/shard_map/ppermute | solution.py:27
  26.3 21.5 %collective-permute-start.5 = (bf16[128,1536]{1,0:T(8,128)(2,1)S(1)}, bf16[128,1536]{1,0:T(8,128)(2,1)S(1)}, u32[]{:S(2)}, u32[]{:S(2)}) collective-permute-start(bf16[128,1536]{1,0:T(8,128)(2,1)S(1)} %convolution_convert_fusion.5), channel_id=1, source_target_pairs={{0,4},{2,6},{4,0},{6,2},{1,5},{3,7},{5,1},{7,3},{8,12},{10,14},{12... | collective-permute-start | bytes 1179656 | tf_op jit(solution)/shard_map/ppermute | solution.py:27
  31.3 15.0 %collective-permute-start.7 = (bf16[128,1536]{1,0:T(8,128)(2,1)S(1)}, bf16[128,1536]{1,0:T(8,128)(2,1)S(1)}, u32[]{:S(2)}, u32[]{:S(2)}) collective-permute-start(bf16[128,1536]{1,0:T(8,128)(2,1)S(1)} %convolution_convert_fusion.2), channel_id=1, source_target_pairs={{0,4},{2,6},{4,0},{6,2},{1,5},{3,7},{5,1},{7,3},{8,12},{10,14},{12... | collective-permute-start | bytes 1179656 | tf_op jit(solution)/shard_map/ppermute | solution.py:27
  32.7 35.5 %collective-permute-start.12 = (bf16[256,1536]{1,0:T(8,128)(2,1)S(1)}, bf16[256,1536]{1,0:T(8,128)(2,1)S(1)}, u32[]{:S(2)}, u32[]{:S(2)}) collective-permute-start(bf16[256,1536]{1,0:T(8,128)(2,1)S(1)} %copy-done.1), channel_id=1, source_target_pairs={{0,2},{2,0},{4,6},{6,4},{1,3},{3,1},{5,7},{7,5},{8,10},{10,8},{12,... | collective-permute-start | bytes 2359304 | tf_op jit(solution)/shard_map/ppermute | solution.py:27
  46.4 12.0 %collective-permute-start.13 = (bf16[128,1536]{1,0:T(8,128)(2,1)S(1)}, bf16[128,1536]{1,0:T(8,128)(2,1)S(1)}, u32[]{:S(2)}, u32[]{:S(2)}) collective-permute-start(bf16[128,1536]{1,0:T(8,128)(2,1)S(1)} %convolution_convert_fusion.3), channel_id=1, source_target_pairs={{0,4},{2,6},{4,0},{6,2},{1,5},{3,7},{5,1},{7,3},{8,12},{10,14},{12... | collective-permute-start | bytes 1179656 | tf_op jit(solution)/shard_map/ppermute | solution.py:27
  47.9 17.6 %collective-permute-start.9 = (bf16[128,1536]{1,0:T(8,128)(2,1)S(1)}, bf16[128,1536]{1,0:T(8,128)(2,1)S(1)}, u32[]{:S(2)}, u32[]{:S(2)}) collective-permute-start(bf16[128,1536]{1,0:T(8,128)(2,1)S(1)} %convolution_convert_fusion.4), channel_id=1, source_target_pairs={{0,4},{2,6},{4,0},{6,2},{1,5},{3,7},{5,1},{7,3},{8,12},{10,14},{12... | collective-permute-start | bytes 1179656 | tf_op jit(solution)/shard_map/ppermute | solution.py:27
  48.5 19.4 %collective-permute-start.6 = (bf16[128,1536]{1,0:T(8,128)(2,1)S(1)}, bf16[128,1536]{1,0:T(8,128)(2,1)S(1)}, u32[]{:S(2)}, u32[]{:S(2)}) collective-permute-start(bf16[128,1536]{1,0:T(8,128)(2,1)S(1)} %get-tuple-element.484), channel_id=1, source_target_pairs={{0,1},{1,0},{2,3},{3,2},{4,5},{5,4},{6,7},{7,6},{8,9},{9,8},{10,11... | collective-permute-start | bytes 1179656 | tf_op jit(solution)/shard_map/ppermute | solution.py:27
  65.6 18.4 %collective-permute-start.10 = (bf16[128,1536]{1,0:T(8,128)(2,1)S(1)}, bf16[128,1536]{1,0:T(8,128)(2,1)S(1)}, u32[]{:S(2)}, u32[]{:S(2)}) collective-permute-start(bf16[128,1536]{1,0:T(8,128)(2,1)S(1)} %get-tuple-element.488), channel_id=1, source_target_pairs={{0,1},{1,0},{2,3},{3,2},{4,5},{5,4},{6,7},{7,6},{8,9},{9,8},{10,11... | collective-permute-start | bytes 1179656 | tf_op jit(solution)/shard_map/ppermute | solution.py:27
  67.1 16.9 %collective-permute-start.14 = (bf16[128,1536]{1,0:T(8,128)(2,1)S(1)}, bf16[128,1536]{1,0:T(8,128)(2,1)S(1)}, u32[]{:S(2)}, u32[]{:S(2)}) collective-permute-start(bf16[128,1536]{1,0:T(8,128)(2,1)S(1)} %get-tuple-element.490), channel_id=1, source_target_pairs={{0,1},{1,0},{2,3},{3,2},{4,5},{5,4},{6,7},{7,6},{8,9},{9,8},{10,11... | collective-permute-start | bytes 1179656 | tf_op jit(solution)/shard_map/ppermute | solution.py:27
  101.1 10.4 %collective-permute-start.22 = (bf16[512,128]{1,0:T(8,128)(2,1)S(1)}, bf16[512,128]{1,0:T(8,128)(2,1)S(1)}, u32[]{:S(2)}, u32[]{:S(2)}) collective-permute-start(bf16[512,128]{1,0:T(8,128)(2,1)S(1)} %get-tuple-element.559), channel_id=1, source_target_pairs={{0,4},{2,6},{4,0},{6,2},{1,5},{3,7},{5,1},{7,3},{8,12},{10,14},{12... | collective-permute-start | bytes 393224 | tf_op jit(solution)/shard_map/ppermute | solution.py:27
  101.6 14.5 %collective-permute-start.25 = (bf16[512,256]{1,0:T(8,128)(2,1)S(1)}, bf16[512,256]{1,0:T(8,128)(2,1)S(1)}, u32[]{:S(2)}, u32[]{:S(2)}) collective-permute-start(bf16[512,256]{1,0:T(8,128)(2,1)S(1)} %pad_maximum_fusion.14), channel_id=1, source_target_pairs={{0,1},{1,0},{2,3},{3,2},{4,5},{5,4},{6,7},{7,6},{8,9},{9,8},{10,11... | collective-permute-start | bytes 786440 | tf_op jit(solution)/shard_map/ppermute | solution.py:27
  107.1 10.7 %collective-permute-start.20 = (bf16[1024,128]{1,0:T(8,128)(2,1)S(1)}, bf16[1024,128]{1,0:T(8,128)(2,1)S(1)}, u32[]{:S(2)}, u32[]{:S(2)}) collective-permute-start(bf16[1024,128]{1,0:T(8,128)(2,1)S(1)} %slice.610), channel_id=1, source_target_pairs={{24,16},{25,17},{26,18},{27,19},{28,20},{29,21},{30,22},{31,23}} | collective-permute-start | bytes 786440 | tf_op jit(solution)/shard_map/ppermute | solution.py:80
  107.7 10.5 %collective-permute-start.19 = (bf16[1024,128]{1,0:T(8,128)(2,1)S(1)}, bf16[1024,128]{1,0:T(8,128)(2,1)S(1)}, u32[]{:S(2)}, u32[]{:S(2)}) collective-permute-start(bf16[1024,128]{1,0:T(8,128)(2,1)S(1)} %slice.610), channel_id=1, source_target_pairs={{0,8},{1,9},{2,10},{3,11},{4,12},{5,13},{6,14},{7,15}} | collective-permute-start | bytes 786440 | tf_op jit(solution)/shard_map/ppermute | solution.py:80
  114.1 13.6 %collective-permute-start.30 = (bf16[1024,128]{1,0:T(8,128)(2,1)S(1)}, bf16[1024,128]{1,0:T(8,128)(2,1)S(1)}, u32[]{:S(2)}, u32[]{:S(2)}) collective-permute-start(bf16[1024,128]{1,0:T(8,128)(2,1)S(1)} %pad_maximum_fusion.16), channel_id=1, source_target_pairs={{24,16},{25,17},{26,18},{27,19},{28,20},{29,21},{30,22},{31,23}} | collective-permute-start | bytes 786440 | tf_op jit(solution)/shard_map/ppermute | solution.py:80
  114.8 12.9 %collective-permute-start.29 = (bf16[1024,128]{1,0:T(8,128)(2,1)S(1)}, bf16[1024,128]{1,0:T(8,128)(2,1)S(1)}, u32[]{:S(2)}, u32[]{:S(2)}) collective-permute-start(bf16[1024,128]{1,0:T(8,128)(2,1)S(1)} %pad_maximum_fusion.16), channel_id=1, source_target_pairs={{0,8},{1,9},{2,10},{3,11},{4,12},{5,13},{6,14},{7,15}} | collective-permute-start | bytes 786440 | tf_op jit(solution)/shard_map/ppermute | solution.py:80
  117.7 27.2 %collective-permute-start.35 = (bf16[512,512]{1,0:T(8,128)(2,1)S(1)}, bf16[512,512]{1,0:T(8,128)(2,1)S(1)}, u32[]{:S(2)}, u32[]{:S(2)}) collective-permute-start(bf16[512,512]{1,0:T(8,128)(2,1)S(1)} %pad_maximum_fusion), channel_id=1, source_target_pairs={{0,1},{1,0},{2,3},{3,2},{4,5},{5,4},{6,7},{7,6},{8,9},{9,8},{10,11... | collective-permute-start | bytes 1572872 | tf_op jit(solution)/shard_map/ppermute | solution.py:27
  118.5 14.5 %collective-permute-start.24 = (bf16[1024,128]{1,0:T(8,128)(2,1)S(1)}, bf16[1024,128]{1,0:T(8,128)(2,1)S(1)}, u32[]{:S(2)}, u32[]{:S(2)}) collective-permute-start(bf16[1024,128]{1,0:T(8,128)(2,1)S(1)} %get-tuple-element.259), channel_id=1, source_target_pairs={{16,8},{24,16},{17,9},{25,17},{18,10},{26,18},{19,11},{27,19},{20,... | collective-permute-start | bytes 786440 | tf_op jit(solution)/shard_map/ppermute | solution.py:80
  122.6 11.3 %collective-permute-start.23 = (bf16[1024,128]{1,0:T(8,128)(2,1)S(1)}, bf16[1024,128]{1,0:T(8,128)(2,1)S(1)}, u32[]{:S(2)}, u32[]{:S(2)}) collective-permute-start(bf16[1024,128]{1,0:T(8,128)(2,1)S(1)} %get-tuple-element.255), channel_id=1, source_target_pairs={{0,8},{8,16},{1,9},{9,17},{2,10},{10,18},{3,11},{11,19},{4,12},{12... | collective-permute-start | bytes 786440 | tf_op jit(solution)/shard_map/ppermute | solution.py:80
  127.9 10.9 %collective-permute-start.32 = (bf16[1024,128]{1,0:T(8,128)(2,1)S(1)}, bf16[1024,128]{1,0:T(8,128)(2,1)S(1)}, u32[]{:S(2)}, u32[]{:S(2)}) collective-permute-start(bf16[1024,128]{1,0:T(8,128)(2,1)S(1)} %get-tuple-element.273), channel_id=1, source_target_pairs={{16,8},{24,16},{17,9},{25,17},{18,10},{26,18},{19,11},{27,19},{20,... | collective-permute-start | bytes 786440 | tf_op jit(solution)/shard_map/ppermute | solution.py:80
  128.6 11.5 %collective-permute-start.31 = (bf16[1024,128]{1,0:T(8,128)(2,1)S(1)}, bf16[1024,128]{1,0:T(8,128)(2,1)S(1)}, u32[]{:S(2)}, u32[]{:S(2)}) collective-permute-start(bf16[1024,128]{1,0:T(8,128)(2,1)S(1)} %get-tuple-element.269), channel_id=1, source_target_pairs={{0,8},{8,16},{1,9},{9,17},{2,10},{10,18},{3,11},{11,19},{4,12},{12... | collective-permute-start | bytes 786440 | tf_op jit(solution)/shard_map/ppermute | solution.py:80
  132.9 21.5 %collective-permute-start.49 = (bf16[512,512]{1,0:T(8,128)(2,1)S(1)}, bf16[512,512]{1,0:T(8,128)(2,1)S(1)}, u32[]{:S(2)}, u32[]{:S(2)}) collective-permute-start(bf16[512,512]{1,0:T(8,128)(2,1)S(1)} %pad_maximum_fusion.1), channel_id=1, source_target_pairs={{0,1},{1,0},{2,3},{3,2},{4,5},{5,4},{6,7},{7,6},{8,9},{9,8},{10,11... | collective-permute-start | bytes 1572872 | tf_op jit(solution)/shard_map/ppermute | solution.py:27
  134.2 12.1 %collective-permute-start.28 = (bf16[1024,128]{1,0:T(8,128)(2,1)S(1)}, bf16[1024,128]{1,0:T(8,128)(2,1)S(1)}, u32[]{:S(2)}, u32[]{:S(2)}) collective-permute-start(bf16[1024,128]{1,0:T(8,128)(2,1)S(1)} %get-tuple-element.281), channel_id=1, source_target_pairs={{0,8},{8,16},{16,24},{1,9},{9,17},{17,25},{2,10},{10,18},{18,26},{... | collective-permute-start | bytes 786440 | tf_op jit(solution)/shard_map/ppermute | solution.py:80
  146.3 13.5 %collective-permute-start.36 = (bf16[512,512]{1,0:T(8,128)(2,1)S(1)}, bf16[512,512]{1,0:T(8,128)(2,1)S(1)}, u32[]{:S(2)}, u32[]{:S(2)}) collective-permute-start(bf16[512,512]{1,0:T(8,128)(2,1)S(1)} %get-tuple-element.495), channel_id=1, source_target_pairs={{0,4},{2,6},{4,0},{6,2},{1,5},{3,7},{5,1},{7,3},{8,12},{10,14},{12... | collective-permute-start | bytes 1572872 | tf_op jit(solution)/shard_map/ppermute | solution.py:27
  154.5 30.9 %collective-permute-start.50 = (bf16[512,512]{1,0:T(8,128)(2,1)S(1)}, bf16[512,512]{1,0:T(8,128)(2,1)S(1)}, u32[]{:S(2)}, u32[]{:S(2)}) collective-permute-start(bf16[512,512]{1,0:T(8,128)(2,1)S(1)} %get-tuple-element.493), channel_id=1, source_target_pairs={{0,4},{2,6},{4,0},{6,2},{1,5},{3,7},{5,1},{7,3},{8,12},{10,14},{12... | collective-permute-start | bytes 1572872 | tf_op jit(solution)/shard_map/ppermute | solution.py:27
  166.2 12.8 %collective-permute-start.40 = (bf16[1024,128]{1,0:T(8,128)(2,1)S(1)}, bf16[1024,128]{1,0:T(8,128)(2,1)S(1)}, u32[]{:S(2)}, u32[]{:S(2)}) collective-permute-start(bf16[1024,128]{1,0:T(8,128)(2,1)S(1)} %get-tuple-element.311), channel_id=1, source_target_pairs={{0,8},{8,16},{16,24},{1,9},{9,17},{17,25},{2,10},{10,18},{18,26},{... | collective-permute-start | bytes 786440 | tf_op jit(solution)/shard_map/ppermute | solution.py:80
  173.1 18.4 %collective-permute-start.38 = (bf16[1024,128]{1,0:T(8,128)(2,1)S(1)}, bf16[1024,128]{1,0:T(8,128)(2,1)S(1)}, u32[]{:S(2)}, u32[]{:S(2)}) collective-permute-start(bf16[1024,128]{1,0:T(8,128)(2,1)S(1)} %get-tuple-element.301), channel_id=1, source_target_pairs={{0,8},{8,16},{16,24},{1,9},{9,17},{17,25},{2,10},{10,18},{18,26},{... | collective-permute-start | bytes 786440 | tf_op jit(solution)/shard_map/ppermute | solution.py:80
  177.6 13.8 %collective-permute-start.37 = (bf16[1024,128]{1,0:T(8,128)(2,1)S(1)}, bf16[1024,128]{1,0:T(8,128)(2,1)S(1)}, u32[]{:S(2)}, u32[]{:S(2)}) collective-permute-start(bf16[1024,128]{1,0:T(8,128)(2,1)S(1)} %get-tuple-element.305), channel_id=1, source_target_pairs={{8,0},{16,8},{24,16},{9,1},{17,9},{25,17},{10,2},{18,10},{26,18},{... | collective-permute-start | bytes 786440 | tf_op jit(solution)/shard_map/ppermute | solution.py:80
  180.3 18.6 %collective-permute-start.44 = (bf16[1024,128]{1,0:T(8,128)(2,1)S(1)}, bf16[1024,128]{1,0:T(8,128)(2,1)S(1)}, u32[]{:S(2)}, u32[]{:S(2)}) collective-permute-start(bf16[1024,128]{1,0:T(8,128)(2,1)S(1)} %get-tuple-element.331), channel_id=1, source_target_pairs={{0,8},{8,16},{16,24},{1,9},{9,17},{17,25},{2,10},{10,18},{18,26},{... | collective-permute-start | bytes 786440 | tf_op jit(solution)/shard_map/ppermute | solution.py:80
  183.8 15.0 %collective-permute-start.43 = (bf16[1024,128]{1,0:T(8,128)(2,1)S(1)}, bf16[1024,128]{1,0:T(8,128)(2,1)S(1)}, u32[]{:S(2)}, u32[]{:S(2)}) collective-permute-start(bf16[1024,128]{1,0:T(8,128)(2,1)S(1)} %get-tuple-element.335), channel_id=1, source_target_pairs={{8,0},{16,8},{24,16},{9,1},{17,9},{25,17},{10,2},{18,10},{26,18},{... | collective-permute-start | bytes 786440 | tf_op jit(solution)/shard_map/ppermute | solution.py:80
  191.7 13.3 %collective-permute-start.42 = (bf16[1024,128]{1,0:T(8,128)(2,1)S(1)}, bf16[1024,128]{1,0:T(8,128)(2,1)S(1)}, u32[]{:S(2)}, u32[]{:S(2)}) collective-permute-start(bf16[1024,128]{1,0:T(8,128)(2,1)S(1)} %get-tuple-element.321), channel_id=1, source_target_pairs={{0,8},{8,16},{16,24},{1,9},{9,17},{17,25},{2,10},{10,18},{18,26},{... | collective-permute-start | bytes 786440 | tf_op jit(solution)/shard_map/ppermute | solution.py:80
  199.1 14.3 %collective-permute-start.48 = (bf16[1024,128]{1,0:T(8,128)(2,1)S(1)}, bf16[1024,128]{1,0:T(8,128)(2,1)S(1)}, u32[]{:S(2)}, u32[]{:S(2)}) collective-permute-start(bf16[1024,128]{1,0:T(8,128)(2,1)S(1)} %get-tuple-element.353), channel_id=1, source_target_pairs={{0,8},{8,16},{16,24},{1,9},{9,17},{17,25},{2,10},{10,18},{18,26},{... | collective-permute-start | bytes 786440 | tf_op jit(solution)/shard_map/ppermute | solution.py:80
  203.7 10.4 %collective-permute-start.47 = (bf16[1024,128]{1,0:T(8,128)(2,1)S(1)}, bf16[1024,128]{1,0:T(8,128)(2,1)S(1)}, u32[]{:S(2)}, u32[]{:S(2)}) collective-permute-start(bf16[1024,128]{1,0:T(8,128)(2,1)S(1)} %get-tuple-element.357), channel_id=1, source_target_pairs={{8,0},{16,8},{24,16},{9,1},{17,9},{25,17},{10,2},{18,10},{26,18},{... | collective-permute-start | bytes 786440 | tf_op jit(solution)/shard_map/ppermute | solution.py:80
  205.4 10.9 %collective-permute-start.46 = (bf16[1024,128]{1,0:T(8,128)(2,1)S(1)}, bf16[1024,128]{1,0:T(8,128)(2,1)S(1)}, u32[]{:S(2)}, u32[]{:S(2)}) collective-permute-start(bf16[1024,128]{1,0:T(8,128)(2,1)S(1)} %get-tuple-element.343), channel_id=1, source_target_pairs={{0,8},{8,16},{16,24},{1,9},{9,17},{17,25},{2,10},{10,18},{18,26},{... | collective-permute-start | bytes 786440 | tf_op jit(solution)/shard_map/ppermute | solution.py:80
  210.0 11.0 %collective-permute-start.45 = (bf16[1024,128]{1,0:T(8,128)(2,1)S(1)}, bf16[1024,128]{1,0:T(8,128)(2,1)S(1)}, u32[]{:S(2)}, u32[]{:S(2)}) collective-permute-start(bf16[1024,128]{1,0:T(8,128)(2,1)S(1)} %get-tuple-element.347), channel_id=1, source_target_pairs={{8,0},{16,8},{24,16},{9,1},{17,9},{25,17},{10,2},{18,10},{26,18},{... | collective-permute-start | bytes 786440 | tf_op jit(solution)/shard_map/ppermute | solution.py:80
  221.3 10.6 %collective-permute-start.54 = (bf16[1024,128]{1,0:T(8,128)(2,1)S(1)}, bf16[1024,128]{1,0:T(8,128)(2,1)S(1)}, u32[]{:S(2)}, u32[]{:S(2)}) collective-permute-start(bf16[1024,128]{1,0:T(8,128)(2,1)S(1)} %get-tuple-element.373), channel_id=1, source_target_pairs={{0,8},{8,16},{16,24},{1,9},{9,17},{17,25},{2,10},{10,18},{18,26},{... | collective-permute-start | bytes 786440 | tf_op jit(solution)/shard_map/ppermute | solution.py:80
  223.4 10.1 %collective-permute-start.53 = (bf16[1024,128]{1,0:T(8,128)(2,1)S(1)}, bf16[1024,128]{1,0:T(8,128)(2,1)S(1)}, u32[]{:S(2)}, u32[]{:S(2)}) collective-permute-start(bf16[1024,128]{1,0:T(8,128)(2,1)S(1)} %get-tuple-element.377), channel_id=1, source_target_pairs={{8,0},{16,8},{24,16},{9,1},{17,9},{25,17},{10,2},{18,10},{26,18},{... | collective-permute-start | bytes 786440 | tf_op jit(solution)/shard_map/ppermute | solution.py:80
  224.9 13.2 %collective-permute-start.52 = (bf16[1024,128]{1,0:T(8,128)(2,1)S(1)}, bf16[1024,128]{1,0:T(8,128)(2,1)S(1)}, u32[]{:S(2)}, u32[]{:S(2)}) collective-permute-start(bf16[1024,128]{1,0:T(8,128)(2,1)S(1)} %get-tuple-element.363), channel_id=1, source_target_pairs={{0,8},{8,16},{16,24},{1,9},{9,17},{17,25},{2,10},{10,18},{18,26},{... | collective-permute-start | bytes 786440 | tf_op jit(solution)/shard_map/ppermute | solution.py:80
  229.5 10.7 %collective-permute-start.51 = (bf16[1024,128]{1,0:T(8,128)(2,1)S(1)}, bf16[1024,128]{1,0:T(8,128)(2,1)S(1)}, u32[]{:S(2)}, u32[]{:S(2)}) collective-permute-start(bf16[1024,128]{1,0:T(8,128)(2,1)S(1)} %get-tuple-element.367), channel_id=1, source_target_pairs={{8,0},{16,8},{24,16},{9,1},{17,9},{25,17},{10,2},{18,10},{26,18},{... | collective-permute-start | bytes 786440 | tf_op jit(solution)/shard_map/ppermute | solution.py:80
  233.7 11.8 %collective-permute-start.58 = (bf16[1024,128]{1,0:T(8,128)(2,1)S(1)}, bf16[1024,128]{1,0:T(8,128)(2,1)S(1)}, u32[]{:S(2)}, u32[]{:S(2)}) collective-permute-start(bf16[1024,128]{1,0:T(8,128)(2,1)S(1)} %get-tuple-element.393), channel_id=1, source_target_pairs={{0,8},{8,16},{16,24},{1,9},{9,17},{17,25},{2,10},{10,18},{18,26},{... | collective-permute-start | bytes 786440 | tf_op jit(solution)/shard_map/ppermute | solution.py:80
  240.5 11.1 %collective-permute-start.56 = (bf16[1024,128]{1,0:T(8,128)(2,1)S(1)}, bf16[1024,128]{1,0:T(8,128)(2,1)S(1)}, u32[]{:S(2)}, u32[]{:S(2)}) collective-permute-start(bf16[1024,128]{1,0:T(8,128)(2,1)S(1)} %get-tuple-element.383), channel_id=1, source_target_pairs={{0,8},{8,16},{16,24},{1,9},{9,17},{17,25},{2,10},{10,18},{18,26},{... | collective-permute-start | bytes 786440 | tf_op jit(solution)/shard_map/ppermute | solution.py:80
  246.2 13.9 %collective-permute-start.62 = (bf16[1024,128]{1,0:T(8,128)(2,1)S(1)}, bf16[1024,128]{1,0:T(8,128)(2,1)S(1)}, u32[]{:S(2)}, u32[]{:S(2)}) collective-permute-start(bf16[1024,128]{1,0:T(8,128)(2,1)S(1)} %get-tuple-element.412), channel_id=1, source_target_pairs={{0,8},{8,16},{16,24},{1,9},{9,17},{17,25},{2,10},{10,18},{18,26},{... | collective-permute-start | bytes 786440 | tf_op jit(solution)/shard_map/ppermute | solution.py:80
  250.3 10.3 %collective-permute-start.61 = (bf16[1024,128]{1,0:T(8,128)(2,1)S(1)}, bf16[1024,128]{1,0:T(8,128)(2,1)S(1)}, u32[]{:S(2)}, u32[]{:S(2)}) collective-permute-start(bf16[1024,128]{1,0:T(8,128)(2,1)S(1)} %get-tuple-element.415), channel_id=1, source_target_pairs={{8,0},{16,8},{24,16},{9,1},{17,9},{25,17},{10,2},{18,10},{26,18},{... | collective-permute-start | bytes 786440 | tf_op jit(solution)/shard_map/ppermute | solution.py:80
  252.6 10.4 %collective-permute-start.60 = (bf16[1024,128]{1,0:T(8,128)(2,1)S(1)}, bf16[1024,128]{1,0:T(8,128)(2,1)S(1)}, u32[]{:S(2)}, u32[]{:S(2)}) collective-permute-start(bf16[1024,128]{1,0:T(8,128)(2,1)S(1)} %get-tuple-element.403), channel_id=1, source_target_pairs={{0,8},{8,16},{16,24},{1,9},{9,17},{17,25},{2,10},{10,18},{18,26},{... | collective-permute-start | bytes 786440 | tf_op jit(solution)/shard_map/ppermute | solution.py:80
  256.6 10.4 %collective-permute-start.59 = (bf16[1024,128]{1,0:T(8,128)(2,1)S(1)}, bf16[1024,128]{1,0:T(8,128)(2,1)S(1)}, u32[]{:S(2)}, u32[]{:S(2)}) collective-permute-start(bf16[1024,128]{1,0:T(8,128)(2,1)S(1)} %get-tuple-element.406), channel_id=1, source_target_pairs={{8,0},{16,8},{24,16},{9,1},{17,9},{25,17},{10,2},{18,10},{26,18},{... | collective-permute-start | bytes 786440 | tf_op jit(solution)/shard_map/ppermute | solution.py:80
  261.6 10.0 %collective-permute-start.65 = (bf16[1024,128]{1,0:T(8,128)(2,1)S(1)}, bf16[1024,128]{1,0:T(8,128)(2,1)S(1)}, u32[]{:S(2)}, u32[]{:S(2)}) collective-permute-start(bf16[1024,128]{1,0:T(8,128)(2,1)S(1)} %get-tuple-element.431), channel_id=1, source_target_pairs={{8,0},{16,8},{9,1},{17,9},{10,2},{18,10},{11,3},{19,11},{12,4},{20... | collective-permute-start | bytes 786440 | tf_op jit(solution)/shard_map/ppermute | solution.py:80
  (33 other events, 333.2 us)
where the time goes:
time: 296 us; the launch traced here: 293 us
  starting transfers between devices  116 us (39%)
  waiting for transfers between devices  101 us (34%)
  matrix products  35.6 us (12%)
  other arithmetic  23.5 us (8%)
  local copies, waits for them, and re-layouts  14.7 us (5%)
    ppermute x44, starting transfers between devices, stage(): lax.ppermute(value, 'island', [(i, i + move) for i in sources])  96 us
    ppermute x27, waiting for transfers between devices, swap(): return lax.ppermute(value, axis, [(i, i ^ bit) for i in range(count)])  67 us
    ppermute x44, waiting for transfers between devices, stage(): lax.ppermute(value, 'island', [(i, i + move) for i in sources])  34.1 us
    dot_general x5, matrix products, body(): lax.dot_general(context_all, d_all, (((0,), (0,)), ((), ())), preferred_e...  20.4 us
    ppermute x27, starting transfers between devices, swap(): return lax.ppermute(value, axis, [(i, i ^ bit) for i in range(count)])  19.9 us
    dot_general x6, matrix products, project(): jnp.dot(block, weight, preferred_element_type=f32).astype(bf16)  15.3 us
    unnamed x24, other arithmetic  11.7 us
    unnamed x25, local copies, waits for them, and re-layouts  6.98 us
  transfers between devices with their start and end apart: 71, of which 28 were waited for; matrix products, arithmetic and copies ran while one was open for 22% of the time, Pallas kernels for 0%

commit v1 on v0

--- a/solution.py
+++ b/solution.py
@@ -119,8 +119,17 @@
             jnp.dot(block, weight, preferred_element_type=f32).astype(bf16)
         )
 
-    far_pieces = [[swap(context[p * rows : (p + 1) * rows], "fsdp", group) for p in range(pieces)]]
+    residual_parts = regroup(residual)
+    cotangent_parts = regroup(cotangent)
+
     near_blocks = [context] + [swap(context, "fsdp", r) for r in range(1, group)]
+    later = tie(context, residual_parts[0], cotangent_parts[0])
+    far_pieces = [
+        [
+            swap((later if p else context)[p * rows : (p + 1) * rows], "fsdp", group)
+            for p in range(pieces)
+        ]
+    ]
     for r in range(1, group):
         far_pieces.append([swap(piece, "fsdp", r) for piece in far_pieces[0]])
     near_out = [project(context)]
@@ -132,10 +141,8 @@
             far_outs.append(swap(issued, "fsdp", group))
         if r + 1 < group:
             near_out.append(project(tie(near_blocks[r + 1], issued)))
-            issued = tie(issued, near_out[-1])
-
-    residual_parts = regroup(residual)
-    cotangent_parts = regroup(cotangent)
+            issued = tie(near_out[-1], *residual_parts, *cotangent_parts)
+
     gain_part = lax.dynamic_slice_in_dim(gain, t * (width // 2) + low * cols, cols).astype(f32)
 
     hidden, weighted, sums = [], [], []
@@ -189,6 +196,16 @@
             found.append(items[k][first:last])
         return found[0] if len(found) == 1 else jnp.concatenate(found, axis=0)
 
+    def at(h, q, x):
+        return (h * group + q) * 2 + x
+
+    square_groups = [[at(h, q, x) for h in (0, 1) for x in (0, 1)] for q in range(group)]
+    ring_pairs, cross_pairs = [], []
+    for q in range(group):
+        ring_pairs += [(at(x, q, x), at(x, q, 1 - x)) for x in (0, 1)]
+        ring_pairs += [(at(1 - x, q, x), at(x, q, x)) for x in (0, 1)]
+        cross_pairs += [(at(1 - x, q, x), at(x, q, 1 - x)) for x in (0, 1)]
+
     parts = []
     added = 0
     pseudos, arrivals = [], []
@@ -203,18 +220,23 @@
             ],
             axis=0,
         ).astype(bf16)
-        if c in (2, 3):
-            d_local = tie(d_local, arrivals[c - 2 if c == 2 else 2])
-        elif c > 3:
-            d_local = tie(d_local, pseudos[c - 2])
-        came = swap(d_local, "tp", 1)
-        if c:
-            came = tie(came, d_sent)
-        arrivals.append(came)
-        d_own = jnp.where(near, d_local, came)
-        d_sent = jnp.where(near, came, d_local)
-        d_far = swap(d_sent, "fsdp", group)
-        d_all = jnp.concatenate([d_own, d_far], axis=0)
+        if wide > 2:
+            if len(arrivals) > 0:
+                d_local = tie(d_local, arrivals[0])
+            blocks = lax.all_gather(
+                d_local, ("fsdp", "tp"), axis_index_groups=square_groups, axis=0, tiled=False
+            )
+            d_near = lax.dynamic_index_in_dim(blocks, 3 * high, 0, keepdims=False)
+            d_far = lax.dynamic_index_in_dim(blocks, 2 - high, 0, keepdims=False)
+        else:
+            if c > 0:
+                d_local = tie(d_local, arrivals[-1])
+            ring = lax.ppermute(d_local, ("fsdp", "tp"), ring_pairs)
+            cross = lax.ppermute(d_local, ("fsdp", "tp"), cross_pairs)
+            arrivals.append(ring)
+            d_near = jnp.where(near, d_local, ring)
+            d_far = jnp.where(near, ring, cross)
+        d_all = jnp.concatenate([d_near, d_far], axis=0)
         grad = lax.dot_general(
             context_all, d_all, (((0,), (0,)), ((), ())), preferred_element_type=f32
         ) / (tok_rows * fsdp_count)

time: 296 us -> 321 us (1.084)
  between operations: 2.14 us -> 16.1 us
  local copies, waits for them, and re-layouts: 14.7 us -> 20.7 us
    ppermute x0 -> x6, starting transfers between devices: none -> 12.8 us  [the longest x3 11 us: body(): cross = lax.ppermute(d_local, ('fsdp', 'tp'), cross_pairs)]
    ppermute x27 -> x17, waiting for transfers between devices: 67 us -> 54.9 us  [swap(): return lax.ppermute(value, axis, [(i, i ^ bit) for i in range(count)])]
    ppermute x0 -> x6, waiting for transfers between devices: none -> 8.45 us  [the longest x3 8.44 us: body(): ring = lax.ppermute(d_local, ('fsdp', 'tp'), ring_pairs)]
    ppermute x27 -> x17, starting transfers between devices: 19.9 us -> 11.6 us  [swap(): return lax.ppermute(value, axis, [(i, i ^ bit) for i in range(count)])]
    dot_general x5, matrix products: 20.4 us -> 25.1 us  [body(): lax.dot_general(context_all, d_all, (((0,), (0,)), ((), ())), preferred_e...]
    ppermute x44, waiting for transfers between devices: 34.1 us -> 38.2 us  [stage(): lax.ppermute(value, 'island', [(i, i + move) for i in sources])]
    unnamed x24 -> x26, other arithmetic: 11.7 us -> 7.87 us
    unnamed x25 -> x91, local copies, waits for them, and re-layouts: 6.98 us -> 8.29 us
  transfers between devices with their start and end apart: 71 -> 69, of which waited for: 28 -> 30; matrix products, arithmetic and copies ran while one was open for 22% -> 20% of each run, Pallas kernels for 0% -> 0%
where the time goes in v1:
time: 321 us; the launch traced here: 317 us
  starting transfers between devices  118 us (37%)
  waiting for transfers between devices  102 us (32%)
  matrix products  37.9 us (12%)
  other arithmetic  22.9 us (7%)
  local copies, waits for them, and re-layouts  20.7 us (6%)
  between operations  16.1 us (5%)
    ppermute x44, starting transfers between devices, stage(): lax.ppermute(value, 'island', [(i, i + move) for i in sources])  93.1 us
    ppermute x17, waiting for transfers between devices, swap(): return lax.ppermute(value, axis, [(i, i ^ bit) for i in range(count)])  54.9 us
    ppermute x44, waiting for transfers between devices, stage(): lax.ppermute(value, 'island', [(i, i + move) for i in sources])  38.2 us
    dot_general x5, matrix products, body(): lax.dot_general(context_all, d_all, (((0,), (0,)), ((), ())), preferred_e...  25.1 us
    dot_general x6, matrix products, project(): jnp.dot(block, weight, preferred_element_type=f32).astype(bf16)  12.8 us
    ppermute x17, starting transfers between devices, swap(): return lax.ppermute(value, axis, [(i, i ^ bit) for i in range(count)])  11.6 us
    ppermute x3, starting transfers between devices, body(): cross = lax.ppermute(d_local, ('fsdp', 'tp'), cross_pairs)  11 us
    ppermute x3, waiting for transfers between devices, body(): ring = lax.ppermute(d_local, ('fsdp', 'tp'), ring_pairs)  8.44 us
  transfers between devices with their start and end apart: 69, of which 30 were waited for; matrix products, arithmetic and copies ran while one was open for 20% of the time, Pallas kernels for 0%

profile of v1, /device:TPU:2, one launch (start us, length us, event | category | flops | bytes accessed | tf_op | source)
XLA Modules:
  0.0 316.7 jit_solution(16523297127202711146)
XLA Ops:
  10.6 2.5 constant_dynamic-slice_fusion.1
  13.3 2.4 constant_dynamic-slice_fusion
  17.0 2.3 convolution_convert_fusion.1
  21.2 3.1 convolution_convert_fusion.5
  25.9 3.8 %collective-permute-done.2 = bf16[128,1536]{1,0:T(8,128)(2,1)} collective-permute-done((bf16[128,1536]{1,0:T(8,128)(2,1)}, bf16[128,1536]{1,0:T(8,128)(2,1)}, u32[]{:S(2)}, u32[]{:S(2)}) %collective-permute-start.2) | collective-permute-done | bytes 393248 | tf_op jit(solution)/shard_map/ppermute | solution.py:27
  29.7 3.2 %convolution_convert_fusion.2 = bf16[128,1536]{1,0:T(8,128)(2,1)S(1)} fusion(bf16[128,1536]{1,0:T(8,128)(2,1)} %collective-permute-done.2, bf16[1536,1536]{1,0:T(8,128)(2,1)} %param.12), kind=kOutput, calls=%fused_computation.20 | convolution fusion | flops 604176384 | bytes 5505024 | tf_op jit(solution)/shard_map/dot_general | solution.py:119
  37.1 9.4 %collective-permute-done.7 = bf16[128,1536]{1,0:T(8,128)(2,1)S(1)} collective-permute-done((bf16[128,1536]{1,0:T(8,128)(2,1)S(1)}, bf16[128,1536]{1,0:T(8,128)(2,1)S(1)}, u32[]{:S(2)}, u32[]{:S(2)}) %collective-permute-start.7) | collective-permute-done | bytes 393248 | tf_op jit(solution)/shard_map/ppermute | solution.py:27
  48.7 2.5 convolution_convert_fusion
  51.3 11.7 %collective-permute-done.13 = bf16[128,1536]{1,0:T(8,128)(2,1)S(1)} collective-permute-done((bf16[128,1536]{1,0:T(8,128)(2,1)S(1)}, bf16[128,1536]{1,0:T(8,128)(2,1)S(1)}, u32[]{:S(2)}, u32[]{:S(2)}) %collective-permute-start.13) | collective-permute-done | bytes 393248 | tf_op jit(solution)/shard_map/ppermute | solution.py:27
  66.3 8.7 %collective-permute-done.8 = bf16[128,1536]{1,0:T(8,128)(2,1)S(1)} collective-permute-done((bf16[128,1536]{1,0:T(8,128)(2,1)S(1)}, bf16[128,1536]{1,0:T(8,128)(2,1)S(1)}, u32[]{:S(2)}, u32[]{:S(2)}) %collective-permute-start.8) | collective-permute-done | bytes 393248 | tf_op jit(solution)/shard_map/ppermute | solution.py:27
  75.4 15.2 %collective-permute-done.14 = bf16[128,1536]{1,0:T(8,128)(2,1)S(1)} collective-permute-done((bf16[128,1536]{1,0:T(8,128)(2,1)S(1)}, bf16[128,1536]{1,0:T(8,128)(2,1)S(1)}, u32[]{:S(2)}, u32[]{:S(2)}) %collective-permute-start.14) | collective-permute-done | bytes 393248 | tf_op jit(solution)/shard_map/ppermute | solution.py:27
  94.5 3.1 collective-permute-done.16
  101.0 2.3 collective-permute-done.17
  105.8 3.4 %collective-permute-start.18 = (bf16[512,128]{1,0:T(8,128)(2,1)S(1)}, bf16[512,128]{1,0:T(8,128)(2,1)S(1)}, u32[]{:S(2)}, u32[]{:S(2)}) collective-permute-start(bf16[512,128]{1,0:T(8,128)(2,1)S(1)} %pad_maximum_fusion.21), channel_id=1, source_target_pairs={{4,1},{1,4},{6,3},{3,6},{12,9},{9,12},{14,11},{11,14},{20,17},{17,... | collective-permute-start | bytes 393224 | tf_op jit(solution)/shard_map/ppermute | solution.py:235
  111.8 3.3 %collective-permute-start.22 = (bf16[512,128]{1,0:T(8,128)(2,1)S(1)}, bf16[512,128]{1,0:T(8,128)(2,1)S(1)}, u32[]{:S(2)}, u32[]{:S(2)}) collective-permute-start(bf16[512,128]{1,0:T(8,128)(2,1)S(1)} %pad_maximum_fusion.22), channel_id=1, source_target_pairs={{4,1},{1,4},{6,3},{3,6},{12,9},{9,12},{14,11},{11,14},{20,17},{17,... | collective-permute-start | bytes 393224 | tf_op jit(solution)/shard_map/ppermute | solution.py:235
  116.1 6.1 %collective-permute-done.21 = bf16[512,128]{1,0:T(8,128)(2,1)S(1)} collective-permute-done((bf16[512,128]{1,0:T(8,128)(2,1)S(1)}, bf16[512,128]{1,0:T(8,128)(2,1)S(1)}, u32[]{:S(2)}, u32[]{:S(2)}) %collective-permute-start.21) | collective-permute-done | bytes 131104 | tf_op jit(solution)/shard_map/ppermute | solution.py:234
  122.2 4.2 %collective-permute-start.26 = (bf16[512,256]{1,0:T(8,128)(2,1)S(1)}, bf16[512,256]{1,0:T(8,128)(2,1)S(1)}, u32[]{:S(2)}, u32[]{:S(2)}) collective-permute-start(bf16[512,256]{1,0:T(8,128)(2,1)S(1)} %pad_maximum_fusion.14), channel_id=1, source_target_pairs={{4,1},{1,4},{6,3},{3,6},{12,9},{9,12},{14,11},{11,14},{20,17},{17,... | collective-permute-start | bytes 786440 | tf_op jit(solution)/shard_map/ppermute | solution.py:235
  126.9 3.8 %fusion.58 = bf16[1536,128]{1,0:T(8,128)(2,1)S(1)} fusion(bf16[1536,1536]{1,0:T(8,128)(2,1)} %param.12, bf16[1,1536,1536]{2,1,0:T(8,128)(2,1)} %param.14, bf16[1,1536,1536]{2,1,0:T(8,128)(2,1)} %param.13, bf16[1024,1536]{1,0:T(8,128)(2,1)} %copy-done.29, bf16[512,128]{1,0:T(8,128)(2,1)S(1)} %get-tuple-element.553, bf16[512,128]{1,0:T(8,128)(2,1)S(1)} %get-tuple-element.552), kind=kOutput, calls=%fused_computation.110 | convolution fusion | flops 406716416 | bytes 4980736 | tf_op jit(solution)/shard_map/dot_general | solution.py:240
  130.7 2.7 fusion.57
  134.2 3.5 %collective-permute-start.29 = (bf16[1024,128]{1,0:T(8,128)(2,1)S(1)}, bf16[1024,128]{1,0:T(8,128)(2,1)S(1)}, u32[]{:S(2)}, u32[]{:S(2)}) collective-permute-start(bf16[1024,128]{1,0:T(8,128)(2,1)S(1)} %pad_maximum_fusion.16), channel_id=1, source_target_pairs={{0,8},{1,9},{2,10},{3,11},{4,12},{5,13},{6,14},{7,15}} | collective-permute-start | bytes 786440 | tf_op jit(solution)/shard_map/ppermute | solution.py:80
  139.7 3.8 %fusion.20 = bf16[1536,256]{1,0:T(8,128)(2,1)S(1)} fusion(bf16[1536,1536]{1,0:T(8,128)(2,1)} %param.12, bf16[1,1536,1536]{2,1,0:T(8,128)(2,1)} %param.14, bf16[1,1536,1536]{2,1,0:T(8,128)(2,1)} %param.13, bf16[1024,1536]{1,0:T(8,128)(2,1)S(1)} %copy-done.30, bf16[512,256]{1,0:T(8,128)(2,1)S(1)} %get-tuple-element.549, ...), kind=kOutput, calls=%fused_computation.32 | convolution fusion | flops 813432832 | bytes 6815744 | tf_op jit(solution)/shard_map/dot_general | solution.py:240
  144.5 3.6 %collective-permute-start.31 = (bf16[1024,128]{1,0:T(8,128)(2,1)S(1)}, bf16[1024,128]{1,0:T(8,128)(2,1)S(1)}, u32[]{:S(2)}, u32[]{:S(2)}) collective-permute-start(bf16[1024,128]{1,0:T(8,128)(2,1)S(1)} %get-tuple-element.267), channel_id=1, source_target_pairs={{0,8},{8,16},{1,9},{9,17},{2,10},{10,18},{3,11},{11,19},{4,12},{12... | collective-permute-start | bytes 786440 | tf_op jit(solution)/shard_map/ppermute | solution.py:80
  149.0 5.2 %collective-permute-start.23 = (bf16[1024,128]{1,0:T(8,128)(2,1)S(1)}, bf16[1024,128]{1,0:T(8,128)(2,1)S(1)}, u32[]{:S(2)}, u32[]{:S(2)}) collective-permute-start(bf16[1024,128]{1,0:T(8,128)(2,1)S(1)} %get-tuple-element.253), channel_id=1, source_target_pairs={{0,8},{8,16},{1,9},{9,17},{2,10},{10,18},{3,11},{11,19},{4,12},{12... | collective-permute-start | bytes 786440 | tf_op jit(solution)/shard_map/ppermute | solution.py:80
  155.0 4.6 %collective-permute-start.34 = (bf16[1024,128]{1,0:T(8,128)(2,1)S(1)}, bf16[1024,128]{1,0:T(8,128)(2,1)S(1)}, u32[]{:S(2)}, u32[]{:S(2)}) collective-permute-start(bf16[1024,128]{1,0:T(8,128)(2,1)S(1)} %get-tuple-element.288), channel_id=1, source_target_pairs={{0,8},{8,16},{16,24},{1,9},{9,17},{17,25},{2,10},{10,18},{18,26},{... | collective-permute-start | bytes 786440 | tf_op jit(solution)/shard_map/ppermute | solution.py:80
  161.2 5.0 %collective-permute-start.28 = (bf16[1024,128]{1,0:T(8,128)(2,1)S(1)}, bf16[1024,128]{1,0:T(8,128)(2,1)S(1)}, u32[]{:S(2)}, u32[]{:S(2)}) collective-permute-start(bf16[1024,128]{1,0:T(8,128)(2,1)S(1)} %get-tuple-element.278), channel_id=1, source_target_pairs={{0,8},{8,16},{16,24},{1,9},{9,17},{17,25},{2,10},{10,18},{18,26},{... | collective-permute-start | bytes 786440 | tf_op jit(solution)/shard_map/ppermute | solution.py:80
  170.1 4.4 %collective-permute-done.27 = bf16[1024,128]{1,0:T(8,128)(2,1)S(1)} collective-permute-done((bf16[1024,128]{1,0:T(8,128)(2,1)S(1)}, bf16[1024,128]{1,0:T(8,128)(2,1)S(1)}, u32[]{:S(2)}, u32[]{:S(2)}) %collective-permute-start.27) | collective-permute-done | bytes 262176 | tf_op jit(solution)/shard_map/ppermute | solution.py:80
  180.1 7.3 %fusion.12 = bf16[1536,512]{1,0:T(8,128)(2,1)S(1)} fusion(bf16[1536,1536]{1,0:T(8,128)(2,1)} %param.12, bf16[1,1536,1536]{2,1,0:T(8,128)(2,1)} %param.14, bf16[1,1536,1536]{2,1,0:T(8,128)(2,1)} %param.13, bf16[1024,1536]{1,0:T(8,128)(2,1)} %copy-done.29, bf16[512,512]{1,0:T(8,128)(2,1)S(1)} %get-tuple-element.447, bf16[512,512]{1,0:T(8,128)(2,1)S(1)} %get-tuple-element.446), kind=kOutput, calls=%fused_computation.16 | convolution fusion | flops 1626865664 | bytes 10485760 | tf_op jit(solution)/shard_map/dot_general | solution.py:240
  190.6 7.5 %fusion.13 = bf16[1536,512]{1,0:T(8,128)(2,1)S(1)} fusion(bf16[1536,1536]{1,0:T(8,128)(2,1)} %param.12, bf16[1,1536,1536]{2,1,0:T(8,128)(2,1)} %param.14, bf16[1,1536,1536]{2,1,0:T(8,128)(2,1)} %param.13, bf16[1024,1536]{1,0:T(8,128)(2,1)} %copy-done.29, bf16[512,512]{1,0:T(8,128)(2,1)S(1)} %get-tuple-element.445, bf16[512,512]{1,0:T(8,128)(2,1)S(1)} %get-tuple-element.444), kind=kOutput, calls=%fused_computation.17 | convolution fusion | flops 1626865664 | bytes 10485760 | tf_op jit(solution)/shard_map/dot_general | solution.py:240
  198.7 4.2 %collective-permute-start.38 = (bf16[1024,128]{1,0:T(8,128)(2,1)S(1)}, bf16[1024,128]{1,0:T(8,128)(2,1)S(1)}, u32[]{:S(2)}, u32[]{:S(2)}) collective-permute-start(bf16[1024,128]{1,0:T(8,128)(2,1)S(1)} %get-tuple-element.308), channel_id=1, source_target_pairs={{0,8},{8,16},{16,24},{1,9},{9,17},{17,25},{2,10},{10,18},{18,26},{... | collective-permute-start | bytes 786440 | tf_op jit(solution)/shard_map/ppermute | solution.py:80
  204.5 4.6 %collective-permute-start.36 = (bf16[1024,128]{1,0:T(8,128)(2,1)S(1)}, bf16[1024,128]{1,0:T(8,128)(2,1)S(1)}, u32[]{:S(2)}, u32[]{:S(2)}) collective-permute-start(bf16[1024,128]{1,0:T(8,128)(2,1)S(1)} %get-tuple-element.298), channel_id=1, source_target_pairs={{0,8},{8,16},{16,24},{1,9},{9,17},{17,25},{2,10},{10,18},{18,26},{... | collective-permute-start | bytes 786440 | tf_op jit(solution)/shard_map/ppermute | solution.py:80
  211.9 3.7 %collective-permute-start.42 = (bf16[1024,128]{1,0:T(8,128)(2,1)S(1)}, bf16[1024,128]{1,0:T(8,128)(2,1)S(1)}, u32[]{:S(2)}, u32[]{:S(2)}) collective-permute-start(bf16[1024,128]{1,0:T(8,128)(2,1)S(1)} %get-tuple-element.328), channel_id=1, source_target_pairs={{0,8},{8,16},{16,24},{1,9},{9,17},{17,25},{2,10},{10,18},{18,26},{... | collective-permute-start | bytes 786440 | tf_op jit(solution)/shard_map/ppermute | solution.py:80
  217.6 4.1 %collective-permute-start.40 = (bf16[1024,128]{1,0:T(8,128)(2,1)S(1)}, bf16[1024,128]{1,0:T(8,128)(2,1)S(1)}, u32[]{:S(2)}, u32[]{:S(2)}) collective-permute-start(bf16[1024,128]{1,0:T(8,128)(2,1)S(1)} %get-tuple-element.318), channel_id=1, source_target_pairs={{0,8},{8,16},{16,24},{1,9},{9,17},{17,25},{2,10},{10,18},{18,26},{... | collective-permute-start | bytes 786440 | tf_op jit(solution)/shard_map/ppermute | solution.py:80
  224.2 4.3 %collective-permute-start.46 = (bf16[1024,128]{1,0:T(8,128)(2,1)S(1)}, bf16[1024,128]{1,0:T(8,128)(2,1)S(1)}, u32[]{:S(2)}, u32[]{:S(2)}) collective-permute-start(bf16[1024,128]{1,0:T(8,128)(2,1)S(1)} %get-tuple-element.349), channel_id=1, source_target_pairs={{0,8},{8,16},{16,24},{1,9},{9,17},{17,25},{2,10},{10,18},{18,26},{... | collective-permute-start | bytes 786440 | tf_op jit(solution)/shard_map/ppermute | solution.py:80
  230.8 4.0 %collective-permute-start.44 = (bf16[1024,128]{1,0:T(8,128)(2,1)S(1)}, bf16[1024,128]{1,0:T(8,128)(2,1)S(1)}, u32[]{:S(2)}, u32[]{:S(2)}) collective-permute-start(bf16[1024,128]{1,0:T(8,128)(2,1)S(1)} %get-tuple-element.339), channel_id=1, source_target_pairs={{0,8},{8,16},{16,24},{1,9},{9,17},{17,25},{2,10},{10,18},{18,26},{... | collective-permute-start | bytes 786440 | tf_op jit(solution)/shard_map/ppermute | solution.py:80
  237.8 3.9 %collective-permute-start.50 = (bf16[1024,128]{1,0:T(8,128)(2,1)S(1)}, bf16[1024,128]{1,0:T(8,128)(2,1)S(1)}, u32[]{:S(2)}, u32[]{:S(2)}) collective-permute-start(bf16[1024,128]{1,0:T(8,128)(2,1)S(1)} %get-tuple-element.369), channel_id=1, source_target_pairs={{0,8},{8,16},{16,24},{1,9},{9,17},{17,25},{2,10},{10,18},{18,26},{... | collective-permute-start | bytes 786440 | tf_op jit(solution)/shard_map/ppermute | solution.py:80
  244.7 3.3 %collective-permute-start.48 = (bf16[1024,128]{1,0:T(8,128)(2,1)S(1)}, bf16[1024,128]{1,0:T(8,128)(2,1)S(1)}, u32[]{:S(2)}, u32[]{:S(2)}) collective-permute-start(bf16[1024,128]{1,0:T(8,128)(2,1)S(1)} %get-tuple-element.359), channel_id=1, source_target_pairs={{0,8},{8,16},{16,24},{1,9},{9,17},{17,25},{2,10},{10,18},{18,26},{... | collective-permute-start | bytes 786440 | tf_op jit(solution)/shard_map/ppermute | solution.py:80
  250.0 2.1 collective-permute-done.49
  252.5 2.4 collective-permute-start.54
  256.2 2.8 collective-permute-done.47
  262.9 2.4 collective-permute-done.53
  265.6 2.2 collective-permute-start.58
  269.1 2.3 collective-permute-done.51
  271.7 2.4 collective-permute-start.56
  279.4 4.2 %collective-permute-done.55 = bf16[1024,128]{1,0:T(8,128)(2,1)S(1)} collective-permute-done((bf16[1024,128]{1,0:T(8,128)(2,1)S(1)}, bf16[1024,128]{1,0:T(8,128)(2,1)S(1)}, u32[]{:S(2)}, u32[]{:S(2)}) %collective-permute-start.55) | collective-permute-done | bytes 262176 | tf_op jit(solution)/shard_map/ppermute | solution.py:80
  286.3 3.5 %collective-permute-done.61 = bf16[1024,128]{1,0:T(8,128)(2,1)S(1)} collective-permute-done((bf16[1024,128]{1,0:T(8,128)(2,1)S(1)}, bf16[1024,128]{1,0:T(8,128)(2,1)S(1)}, u32[]{:S(2)}, u32[]{:S(2)}) %collective-permute-start.61) | collective-permute-done | bytes 262176 | tf_op jit(solution)/shard_map/ppermute | solution.py:80
  296.7 2.2 collective-permute-done.65
  298.9 4.3 %collective-permute-done.63 = bf16[1024,128]{1,0:T(8,128)(2,1)S(1)} collective-permute-done((bf16[1024,128]{1,0:T(8,128)(2,1)S(1)}, bf16[1024,128]{1,0:T(8,128)(2,1)S(1)}, u32[]{:S(2)}, u32[]{:S(2)}) %collective-permute-start.63) | collective-permute-done | bytes 262176 | tf_op jit(solution)/shard_map/ppermute | solution.py:80
  306.1 3.7 %copy-done.31 = f32[1536,1536]{1,0:T(8,128)} copy-done((f32[1536,1536]{1,0:T(8,128)}, f32[1536,1536]{1,0:T(8,128)S(1)}, u32[]{:S(2)}) %copy-start.31) | copy-done | bytes 9437208
  (321 shorter events, 95.5 us)
Async XLA Ops:
  7.2 171.6 %all-gather.5.cloned.1.call-start = ((), (), s32[]{:S(2)}) async-start(), calls=%async_computation | async-start | bytes 2621440 | tf_op jit(solution)/shard_map/all_gather | solution.py:226
  7.2 28.2 %collective-permute-start = (bf16[256,1536]{1,0:T(8,128)(2,1)}, bf16[256,1536]{1,0:T(8,128)(2,1)}, u32[]{:S(2)}, u32[]{:S(2)}) collective-permute-start(bf16[256,1536]{1,0:T(8,128)(2,1)} %param.8), channel_id=1, source_target_pairs={{0,2},{2,0},{4,6},{6,4},{1,3},{3,1},{5,7},{7,5},{8,10},{10,8},{12,... | collective-permute-start | bytes 2359304 | tf_op jit(solution)/shard_map/ppermute | solution.py:27
  9.1 12.1 %collective-permute-start.1 = (bf16[128,1536]{1,0:T(8,128)(2,1)}, bf16[128,1536]{1,0:T(8,128)(2,1)S(1)}, u32[]{:S(2)}, u32[]{:S(2)}) collective-permute-start(bf16[128,1536]{1,0:T(8,128)(2,1)} %slice.463), channel_id=1, source_target_pairs={{0,4},{2,6},{4,0},{6,2},{1,5},{3,7},{5,1},{7,3},{8,12},{10,14},{12... | collective-permute-start | bytes 1179656 | tf_op jit(solution)/shard_map/ppermute | solution.py:27
  13.1 62.2 %collective-permute-start.11 = (bf16[256,1536]{1,0:T(8,128)(2,1)}, bf16[256,1536]{1,0:T(8,128)(2,1)}, u32[]{:S(2)}, u32[]{:S(2)}) collective-permute-start(bf16[256,1536]{1,0:T(8,128)(2,1)} %get-tuple-element.482), channel_id=1, source_target_pairs={{0,2},{2,0},{4,6},{6,4},{1,3},{3,1},{5,7},{7,5},{8,10},{10,8},{12,... | collective-permute-start | bytes 2359304 | tf_op jit(solution)/shard_map/ppermute | solution.py:27
  16.5 13.3 %collective-permute-start.2 = (bf16[128,1536]{1,0:T(8,128)(2,1)}, bf16[128,1536]{1,0:T(8,128)(2,1)}, u32[]{:S(2)}, u32[]{:S(2)}) collective-permute-start(bf16[128,1536]{1,0:T(8,128)(2,1)} %slice.464), channel_id=1, source_target_pairs={{0,4},{2,6},{4,0},{6,2},{1,5},{3,7},{5,1},{7,3},{8,12},{10,14},{12... | collective-permute-start | bytes 1179656 | tf_op jit(solution)/shard_map/ppermute | solution.py:27
  21.2 11.8 %collective-permute-start.3 = (bf16[128,1536]{1,0:T(8,128)(2,1)S(1)}, bf16[128,1536]{1,0:T(8,128)(2,1)S(1)}, u32[]{:S(2)}, u32[]{:S(2)}) collective-permute-start(bf16[128,1536]{1,0:T(8,128)(2,1)S(1)} %collective-permute-done.1), channel_id=1, source_target_pairs={{0,2},{2,0},{4,6},{6,4},{1,3},{3,1},{5,7},{7,5},{8,10},{10,8},{12,... | collective-permute-start | bytes 1179656 | tf_op jit(solution)/shard_map/ppermute | solution.py:27
  24.3 23.7 %collective-permute-start.5 = (bf16[128,1536]{1,0:T(8,128)(2,1)S(1)}, bf16[128,1536]{1,0:T(8,128)(2,1)S(1)}, u32[]{:S(2)}, u32[]{:S(2)}) collective-permute-start(bf16[128,1536]{1,0:T(8,128)(2,1)S(1)} %convolution_convert_fusion.5), channel_id=1, source_target_pairs={{0,4},{2,6},{4,0},{6,2},{1,5},{3,7},{5,1},{7,3},{8,12},{10,14},{12... | collective-permute-start | bytes 1179656 | tf_op jit(solution)/shard_map/ppermute | solution.py:27
  33.0 13.5 %collective-permute-start.7 = (bf16[128,1536]{1,0:T(8,128)(2,1)S(1)}, bf16[128,1536]{1,0:T(8,128)(2,1)S(1)}, u32[]{:S(2)}, u32[]{:S(2)}) collective-permute-start(bf16[128,1536]{1,0:T(8,128)(2,1)S(1)} %convolution_convert_fusion.2), channel_id=1, source_target_pairs={{0,4},{2,6},{4,0},{6,2},{1,5},{3,7},{5,1},{7,3},{8,12},{10,14},{12... | collective-permute-start | bytes 1179656 | tf_op jit(solution)/shard_map/ppermute | solution.py:27
  35.5 39.9 %collective-permute-start.12 = (bf16[256,1536]{1,0:T(8,128)(2,1)S(1)}, bf16[256,1536]{1,0:T(8,128)(2,1)S(1)}, u32[]{:S(2)}, u32[]{:S(2)}) collective-permute-start(bf16[256,1536]{1,0:T(8,128)(2,1)S(1)} %copy-done.23), channel_id=1, source_target_pairs={{0,2},{2,0},{4,6},{6,4},{1,3},{3,1},{5,7},{7,5},{8,10},{10,8},{12,... | collective-permute-start | bytes 2359304 | tf_op jit(solution)/shard_map/ppermute | solution.py:27
  35.8 27.5 %collective-permute-start.9 = (bf16[128,1536]{1,0:T(8,128)(2,1)S(1)}, bf16[128,1536]{1,0:T(8,128)(2,1)S(1)}, u32[]{:S(2)}, u32[]{:S(2)}) collective-permute-start(bf16[128,1536]{1,0:T(8,128)(2,1)S(1)} %convolution_convert_fusion.4), channel_id=1, source_target_pairs={{0,4},{2,6},{4,0},{6,2},{1,5},{3,7},{5,1},{7,3},{8,12},{10,14},{12... | collective-permute-start | bytes 1179656 | tf_op jit(solution)/shard_map/ppermute | solution.py:27
  46.5 16.5 %collective-permute-start.13 = (bf16[128,1536]{1,0:T(8,128)(2,1)S(1)}, bf16[128,1536]{1,0:T(8,128)(2,1)S(1)}, u32[]{:S(2)}, u32[]{:S(2)}) collective-permute-start(bf16[128,1536]{1,0:T(8,128)(2,1)S(1)} %convolution_convert_fusion.3), channel_id=1, source_target_pairs={{0,4},{2,6},{4,0},{6,2},{1,5},{3,7},{5,1},{7,3},{8,12},{10,14},{12... | collective-permute-start | bytes 1179656 | tf_op jit(solution)/shard_map/ppermute | solution.py:27
  48.1 17.1 %collective-permute-start.6 = (bf16[128,1536]{1,0:T(8,128)(2,1)S(1)}, bf16[128,1536]{1,0:T(8,128)(2,1)S(1)}, u32[]{:S(2)}, u32[]{:S(2)}) collective-permute-start(bf16[128,1536]{1,0:T(8,128)(2,1)S(1)} %get-tuple-element.484), channel_id=1, source_target_pairs={{0,1},{1,0},{2,3},{3,2},{4,5},{5,4},{6,7},{7,6},{8,9},{9,8},{10,11... | collective-permute-start | bytes 1179656 | tf_op jit(solution)/shard_map/ppermute | solution.py:27
  62.9 12.0 %collective-permute-start.8 = (bf16[128,1536]{1,0:T(8,128)(2,1)S(1)}, bf16[128,1536]{1,0:T(8,128)(2,1)S(1)}, u32[]{:S(2)}, u32[]{:S(2)}) collective-permute-start(bf16[128,1536]{1,0:T(8,128)(2,1)S(1)} %get-tuple-element.486), channel_id=1, source_target_pairs={{0,1},{1,0},{2,3},{3,2},{4,5},{5,4},{6,7},{7,6},{8,9},{9,8},{10,11... | collective-permute-start | bytes 1179656 | tf_op jit(solution)/shard_map/ppermute | solution.py:27
  63.3 27.2 %collective-permute-start.10 = (bf16[128,1536]{1,0:T(8,128)(2,1)S(1)}, bf16[128,1536]{1,0:T(8,128)(2,1)S(1)}, u32[]{:S(2)}, u32[]{:S(2)}) collective-permute-start(bf16[128,1536]{1,0:T(8,128)(2,1)S(1)} %get-tuple-element.488), channel_id=1, source_target_pairs={{0,1},{1,0},{2,3},{3,2},{4,5},{5,4},{6,7},{7,6},{8,9},{9,8},{10,11... | collective-permute-start | bytes 1179656 | tf_op jit(solution)/shard_map/ppermute | solution.py:27
  65.2 25.4 %collective-permute-start.14 = (bf16[128,1536]{1,0:T(8,128)(2,1)S(1)}, bf16[128,1536]{1,0:T(8,128)(2,1)S(1)}, u32[]{:S(2)}, u32[]{:S(2)}) collective-permute-start(bf16[128,1536]{1,0:T(8,128)(2,1)S(1)} %get-tuple-element.490), channel_id=1, source_target_pairs={{0,1},{1,0},{2,3},{3,2},{4,5},{5,4},{6,7},{7,6},{8,9},{9,8},{10,11... | collective-permute-start | bytes 1179656 | tf_op jit(solution)/shard_map/ppermute | solution.py:27
  103.4 85.8 %all-gather.7.cloned.1.call-start = ((), (), s32[]{:S(2)}) async-start(), calls=%async_computation.1 | async-start | bytes 2621440 | tf_op jit(solution)/shard_map/all_gather | solution.py:226
  105.8 20.9 %collective-permute-start.18 = (bf16[512,128]{1,0:T(8,128)(2,1)S(1)}, bf16[512,128]{1,0:T(8,128)(2,1)S(1)}, u32[]{:S(2)}, u32[]{:S(2)}) collective-permute-start(bf16[512,128]{1,0:T(8,128)(2,1)S(1)} %pad_maximum_fusion.21), channel_id=1, source_target_pairs={{4,1},{1,4},{6,3},{3,6},{12,9},{9,12},{14,11},{11,14},{20,17},{17,... | collective-permute-start | bytes 393224 | tf_op jit(solution)/shard_map/ppermute | solution.py:235
  111.8 14.9 %collective-permute-start.22 = (bf16[512,128]{1,0:T(8,128)(2,1)S(1)}, bf16[512,128]{1,0:T(8,128)(2,1)S(1)}, u32[]{:S(2)}, u32[]{:S(2)}) collective-permute-start(bf16[512,128]{1,0:T(8,128)(2,1)S(1)} %pad_maximum_fusion.22), channel_id=1, source_target_pairs={{4,1},{1,4},{6,3},{3,6},{12,9},{9,12},{14,11},{11,14},{20,17},{17,... | collective-permute-start | bytes 393224 | tf_op jit(solution)/shard_map/ppermute | solution.py:235
  122.2 16.1 %collective-permute-start.26 = (bf16[512,256]{1,0:T(8,128)(2,1)S(1)}, bf16[512,256]{1,0:T(8,128)(2,1)S(1)}, u32[]{:S(2)}, u32[]{:S(2)}) collective-permute-start(bf16[512,256]{1,0:T(8,128)(2,1)S(1)} %pad_maximum_fusion.14), channel_id=1, source_target_pairs={{4,1},{1,4},{6,3},{3,6},{12,9},{9,12},{14,11},{11,14},{20,17},{17,... | collective-permute-start | bytes 786440 | tf_op jit(solution)/shard_map/ppermute | solution.py:235
  126.5 13.2 %collective-permute-start.25 = (bf16[512,256]{1,0:T(8,128)(2,1)S(1)}, bf16[512,256]{1,0:T(8,128)(2,1)S(1)}, u32[]{:S(2)}, u32[]{:S(2)}) collective-permute-start(bf16[512,256]{1,0:T(8,128)(2,1)S(1)} %pad_maximum_fusion.14), channel_id=1, source_target_pairs={{0,1},{5,4},{4,0},{1,5},{2,3},{7,6},{6,2},{3,7},{8,9},{13,12},{12,... | collective-permute-start | bytes 786440 | tf_op jit(solution)/shard_map/ppermute | solution.py:234
  133.5 10.1 %collective-permute-start.30 = (bf16[1024,128]{1,0:T(8,128)(2,1)S(1)}, bf16[1024,128]{1,0:T(8,128)(2,1)S(1)}, u32[]{:S(2)}, u32[]{:S(2)}) collective-permute-start(bf16[1024,128]{1,0:T(8,128)(2,1)S(1)} %pad_maximum_fusion.16), channel_id=1, source_target_pairs={{24,16},{25,17},{26,18},{27,19},{28,20},{29,21},{30,22},{31,23}} | collective-permute-start | bytes 786440 | tf_op jit(solution)/shard_map/ppermute | solution.py:80
  134.2 9.4 %collective-permute-start.29 = (bf16[1024,128]{1,0:T(8,128)(2,1)S(1)}, bf16[1024,128]{1,0:T(8,128)(2,1)S(1)}, u32[]{:S(2)}, u32[]{:S(2)}) collective-permute-start(bf16[1024,128]{1,0:T(8,128)(2,1)S(1)} %pad_maximum_fusion.16), channel_id=1, source_target_pairs={{0,8},{1,9},{2,10},{3,11},{4,12},{5,13},{6,14},{7,15}} | collective-permute-start | bytes 786440 | tf_op jit(solution)/shard_map/ppermute | solution.py:80
  137.7 10.4 %collective-permute-start.20 = (bf16[1024,128]{1,0:T(8,128)(2,1)S(1)}, bf16[1024,128]{1,0:T(8,128)(2,1)S(1)}, u32[]{:S(2)}, u32[]{:S(2)}) collective-permute-start(bf16[1024,128]{1,0:T(8,128)(2,1)S(1)} %slice.610), channel_id=1, source_target_pairs={{24,16},{25,17},{26,18},{27,19},{28,20},{29,21},{30,22},{31,23}} | collective-permute-start | bytes 786440 | tf_op jit(solution)/shard_map/ppermute | solution.py:80
  138.4 9.7 %collective-permute-start.19 = (bf16[1024,128]{1,0:T(8,128)(2,1)S(1)}, bf16[1024,128]{1,0:T(8,128)(2,1)S(1)}, u32[]{:S(2)}, u32[]{:S(2)}) collective-permute-start(bf16[1024,128]{1,0:T(8,128)(2,1)S(1)} %slice.610), channel_id=1, source_target_pairs={{0,8},{1,9},{2,10},{3,11},{4,12},{5,13},{6,14},{7,15}} | collective-permute-start | bytes 786440 | tf_op jit(solution)/shard_map/ppermute | solution.py:80
  143.8 10.4 %collective-permute-start.32 = (bf16[1024,128]{1,0:T(8,128)(2,1)S(1)}, bf16[1024,128]{1,0:T(8,128)(2,1)S(1)}, u32[]{:S(2)}, u32[]{:S(2)}) collective-permute-start(bf16[1024,128]{1,0:T(8,128)(2,1)S(1)} %get-tuple-element.271), channel_id=1, source_target_pairs={{16,8},{24,16},{17,9},{25,17},{18,10},{26,18},{19,11},{27,19},{20,... | collective-permute-start | bytes 786440 | tf_op jit(solution)/shard_map/ppermute | solution.py:80
  144.5 10.2 %collective-permute-start.31 = (bf16[1024,128]{1,0:T(8,128)(2,1)S(1)}, bf16[1024,128]{1,0:T(8,128)(2,1)S(1)}, u32[]{:S(2)}, u32[]{:S(2)}) collective-permute-start(bf16[1024,128]{1,0:T(8,128)(2,1)S(1)} %get-tuple-element.267), channel_id=1, source_target_pairs={{0,8},{8,16},{1,9},{9,17},{2,10},{10,18},{3,11},{11,19},{4,12},{12... | collective-permute-start | bytes 786440 | tf_op jit(solution)/shard_map/ppermute | solution.py:80
  148.3 12.6 %collective-permute-start.24 = (bf16[1024,128]{1,0:T(8,128)(2,1)S(1)}, bf16[1024,128]{1,0:T(8,128)(2,1)S(1)}, u32[]{:S(2)}, u32[]{:S(2)}) collective-permute-start(bf16[1024,128]{1,0:T(8,128)(2,1)S(1)} %get-tuple-element.257), channel_id=1, source_target_pairs={{16,8},{24,16},{17,9},{25,17},{18,10},{26,18},{19,11},{27,19},{20,... | collective-permute-start | bytes 786440 | tf_op jit(solution)/shard_map/ppermute | solution.py:80
  149.0 11.9 %collective-permute-start.23 = (bf16[1024,128]{1,0:T(8,128)(2,1)S(1)}, bf16[1024,128]{1,0:T(8,128)(2,1)S(1)}, u32[]{:S(2)}, u32[]{:S(2)}) collective-permute-start(bf16[1024,128]{1,0:T(8,128)(2,1)S(1)} %get-tuple-element.253), channel_id=1, source_target_pairs={{0,8},{8,16},{1,9},{9,17},{2,10},{10,18},{3,11},{11,19},{4,12},{12... | collective-permute-start | bytes 786440 | tf_op jit(solution)/shard_map/ppermute | solution.py:80
  155.0 12.8 %collective-permute-start.34 = (bf16[1024,128]{1,0:T(8,128)(2,1)S(1)}, bf16[1024,128]{1,0:T(8,128)(2,1)S(1)}, u32[]{:S(2)}, u32[]{:S(2)}) collective-permute-start(bf16[1024,128]{1,0:T(8,128)(2,1)S(1)} %get-tuple-element.288), channel_id=1, source_target_pairs={{0,8},{8,16},{16,24},{1,9},{9,17},{17,25},{2,10},{10,18},{18,26},{... | collective-permute-start | bytes 786440 | tf_op jit(solution)/shard_map/ppermute | solution.py:80
  198.7 12.0 %collective-permute-start.38 = (bf16[1024,128]{1,0:T(8,128)(2,1)S(1)}, bf16[1024,128]{1,0:T(8,128)(2,1)S(1)}, u32[]{:S(2)}, u32[]{:S(2)}) collective-permute-start(bf16[1024,128]{1,0:T(8,128)(2,1)S(1)} %get-tuple-element.308), channel_id=1, source_target_pairs={{0,8},{8,16},{16,24},{1,9},{9,17},{17,25},{2,10},{10,18},{18,26},{... | collective-permute-start | bytes 786440 | tf_op jit(solution)/shard_map/ppermute | solution.py:80
  204.5 12.4 %collective-permute-start.36 = (bf16[1024,128]{1,0:T(8,128)(2,1)S(1)}, bf16[1024,128]{1,0:T(8,128)(2,1)S(1)}, u32[]{:S(2)}, u32[]{:S(2)}) collective-permute-start(bf16[1024,128]{1,0:T(8,128)(2,1)S(1)} %get-tuple-element.298), channel_id=1, source_target_pairs={{0,8},{8,16},{16,24},{1,9},{9,17},{17,25},{2,10},{10,18},{18,26},{... | collective-permute-start | bytes 786440 | tf_op jit(solution)/shard_map/ppermute | solution.py:80
  211.9 11.8 %collective-permute-start.42 = (bf16[1024,128]{1,0:T(8,128)(2,1)S(1)}, bf16[1024,128]{1,0:T(8,128)(2,1)S(1)}, u32[]{:S(2)}, u32[]{:S(2)}) collective-permute-start(bf16[1024,128]{1,0:T(8,128)(2,1)S(1)} %get-tuple-element.328), channel_id=1, source_target_pairs={{0,8},{8,16},{16,24},{1,9},{9,17},{17,25},{2,10},{10,18},{18,26},{... | collective-permute-start | bytes 786440 | tf_op jit(solution)/shard_map/ppermute | solution.py:80
  217.6 12.2 %collective-permute-start.40 = (bf16[1024,128]{1,0:T(8,128)(2,1)S(1)}, bf16[1024,128]{1,0:T(8,128)(2,1)S(1)}, u32[]{:S(2)}, u32[]{:S(2)}) collective-permute-start(bf16[1024,128]{1,0:T(8,128)(2,1)S(1)} %get-tuple-element.318), channel_id=1, source_target_pairs={{0,8},{8,16},{16,24},{1,9},{9,17},{17,25},{2,10},{10,18},{18,26},{... | collective-permute-start | bytes 786440 | tf_op jit(solution)/shard_map/ppermute | solution.py:80
  224.2 12.7 %collective-permute-start.46 = (bf16[1024,128]{1,0:T(8,128)(2,1)S(1)}, bf16[1024,128]{1,0:T(8,128)(2,1)S(1)}, u32[]{:S(2)}, u32[]{:S(2)}) collective-permute-start(bf16[1024,128]{1,0:T(8,128)(2,1)S(1)} %get-tuple-element.349), channel_id=1, source_target_pairs={{0,8},{8,16},{16,24},{1,9},{9,17},{17,25},{2,10},{10,18},{18,26},{... | collective-permute-start | bytes 786440 | tf_op jit(solution)/shard_map/ppermute | solution.py:80
  230.8 12.3 %collective-permute-start.44 = (bf16[1024,128]{1,0:T(8,128)(2,1)S(1)}, bf16[1024,128]{1,0:T(8,128)(2,1)S(1)}, u32[]{:S(2)}, u32[]{:S(2)}) collective-permute-start(bf16[1024,128]{1,0:T(8,128)(2,1)S(1)} %get-tuple-element.339), channel_id=1, source_target_pairs={{0,8},{8,16},{16,24},{1,9},{9,17},{17,25},{2,10},{10,18},{18,26},{... | collective-permute-start | bytes 786440 | tf_op jit(solution)/shard_map/ppermute | solution.py:80
  234.8 9.6 %collective-permute-start.43 = (bf16[1024,128]{1,0:T(8,128)(2,1)S(1)}, bf16[1024,128]{1,0:T(8,128)(2,1)S(1)}, u32[]{:S(2)}, u32[]{:S(2)}) collective-permute-start(bf16[1024,128]{1,0:T(8,128)(2,1)S(1)} %get-tuple-element.343), channel_id=1, source_target_pairs={{8,0},{16,8},{24,16},{9,1},{17,9},{25,17},{10,2},{18,10},{26,18},{... | collective-permute-start | bytes 786440 | tf_op jit(solution)/shard_map/ppermute | solution.py:80
  237.8 12.2 %collective-permute-start.50 = (bf16[1024,128]{1,0:T(8,128)(2,1)S(1)}, bf16[1024,128]{1,0:T(8,128)(2,1)S(1)}, u32[]{:S(2)}, u32[]{:S(2)}) collective-permute-start(bf16[1024,128]{1,0:T(8,128)(2,1)S(1)} %get-tuple-element.369), channel_id=1, source_target_pairs={{0,8},{8,16},{16,24},{1,9},{9,17},{17,25},{2,10},{10,18},{18,26},{... | collective-permute-start | bytes 786440 | tf_op jit(solution)/shard_map/ppermute | solution.py:80
  241.8 10.4 %collective-permute-start.49 = (bf16[1024,128]{1,0:T(8,128)(2,1)S(1)}, bf16[1024,128]{1,0:T(8,128)(2,1)S(1)}, u32[]{:S(2)}, u32[]{:S(2)}) collective-permute-start(bf16[1024,128]{1,0:T(8,128)(2,1)S(1)} %get-tuple-element.373), channel_id=1, source_target_pairs={{8,0},{16,8},{24,16},{9,1},{17,9},{25,17},{10,2},{18,10},{26,18},{... | collective-permute-start | bytes 786440 | tf_op jit(solution)/shard_map/ppermute | solution.py:80
  244.7 11.5 %collective-permute-start.48 = (bf16[1024,128]{1,0:T(8,128)(2,1)S(1)}, bf16[1024,128]{1,0:T(8,128)(2,1)S(1)}, u32[]{:S(2)}, u32[]{:S(2)}) collective-permute-start(bf16[1024,128]{1,0:T(8,128)(2,1)S(1)} %get-tuple-element.359), channel_id=1, source_target_pairs={{0,8},{8,16},{16,24},{1,9},{9,17},{17,25},{2,10},{10,18},{18,26},{... | collective-permute-start | bytes 786440 | tf_op jit(solution)/shard_map/ppermute | solution.py:80
  248.0 11.0 %collective-permute-start.47 = (bf16[1024,128]{1,0:T(8,128)(2,1)S(1)}, bf16[1024,128]{1,0:T(8,128)(2,1)S(1)}, u32[]{:S(2)}, u32[]{:S(2)}) collective-permute-start(bf16[1024,128]{1,0:T(8,128)(2,1)S(1)} %get-tuple-element.363), channel_id=1, source_target_pairs={{8,0},{16,8},{24,16},{9,1},{17,9},{25,17},{10,2},{18,10},{26,18},{... | collective-permute-start | bytes 786440 | tf_op jit(solution)/shard_map/ppermute | solution.py:80
  252.5 10.4 %collective-permute-start.54 = (bf16[1024,128]{1,0:T(8,128)(2,1)S(1)}, bf16[1024,128]{1,0:T(8,128)(2,1)S(1)}, u32[]{:S(2)}, u32[]{:S(2)}) collective-permute-start(bf16[1024,128]{1,0:T(8,128)(2,1)S(1)} %get-tuple-element.389), channel_id=1, source_target_pairs={{0,8},{8,16},{16,24},{1,9},{9,17},{17,25},{2,10},{10,18},{18,26},{... | collective-permute-start | bytes 786440 | tf_op jit(solution)/shard_map/ppermute | solution.py:80
  254.9 10.4 %collective-permute-start.53 = (bf16[1024,128]{1,0:T(8,128)(2,1)S(1)}, bf16[1024,128]{1,0:T(8,128)(2,1)S(1)}, u32[]{:S(2)}, u32[]{:S(2)}) collective-permute-start(bf16[1024,128]{1,0:T(8,128)(2,1)S(1)} %get-tuple-element.393), channel_id=1, source_target_pairs={{8,0},{16,8},{24,16},{9,1},{17,9},{25,17},{10,2},{18,10},{26,18},{... | collective-permute-start | bytes 786440 | tf_op jit(solution)/shard_map/ppermute | solution.py:80
  259.3 9.7 %collective-permute-start.52 = (bf16[1024,128]{1,0:T(8,128)(2,1)S(1)}, bf16[1024,128]{1,0:T(8,128)(2,1)S(1)}, u32[]{:S(2)}, u32[]{:S(2)}) collective-permute-start(bf16[1024,128]{1,0:T(8,128)(2,1)S(1)} %get-tuple-element.379), channel_id=1, source_target_pairs={{0,8},{8,16},{16,24},{1,9},{9,17},{17,25},{2,10},{10,18},{18,26},{... | collective-permute-start | bytes 786440 | tf_op jit(solution)/shard_map/ppermute | solution.py:80
  261.1 10.3 %collective-permute-start.51 = (bf16[1024,128]{1,0:T(8,128)(2,1)S(1)}, bf16[1024,128]{1,0:T(8,128)(2,1)S(1)}, u32[]{:S(2)}, u32[]{:S(2)}) collective-permute-start(bf16[1024,128]{1,0:T(8,128)(2,1)S(1)} %get-tuple-element.383), channel_id=1, source_target_pairs={{8,0},{16,8},{24,16},{9,1},{17,9},{25,17},{10,2},{18,10},{26,18},{... | collective-permute-start | bytes 786440 | tf_op jit(solution)/shard_map/ppermute | solution.py:80
  265.6 10.7 %collective-permute-start.58 = (bf16[1024,128]{1,0:T(8,128)(2,1)S(1)}, bf16[1024,128]{1,0:T(8,128)(2,1)S(1)}, u32[]{:S(2)}, u32[]{:S(2)}) collective-permute-start(bf16[1024,128]{1,0:T(8,128)(2,1)S(1)} %get-tuple-element.408), channel_id=1, source_target_pairs={{0,8},{8,16},{16,24},{1,9},{9,17},{17,25},{2,10},{10,18},{18,26},{... | collective-permute-start | bytes 786440 | tf_op jit(solution)/shard_map/ppermute | solution.py:80
  274.1 9.5 %collective-permute-start.55 = (bf16[1024,128]{1,0:T(8,128)(2,1)S(1)}, bf16[1024,128]{1,0:T(8,128)(2,1)S(1)}, u32[]{:S(2)}, u32[]{:S(2)}) collective-permute-start(bf16[1024,128]{1,0:T(8,128)(2,1)S(1)} %get-tuple-element.402), channel_id=1, source_target_pairs={{8,0},{16,8},{24,16},{9,1},{17,9},{25,17},{10,2},{18,10},{26,18},{... | collective-permute-start | bytes 786440 | tf_op jit(solution)/shard_map/ppermute | solution.py:80
  278.1 11.7 %collective-permute-start.61 = (bf16[1024,128]{1,0:T(8,128)(2,1)S(1)}, bf16[1024,128]{1,0:T(8,128)(2,1)S(1)}, u32[]{:S(2)}, u32[]{:S(2)}) collective-permute-start(bf16[1024,128]{1,0:T(8,128)(2,1)S(1)} %get-tuple-element.427), channel_id=1, source_target_pairs={{8,0},{16,8},{9,1},{17,9},{10,2},{18,10},{11,3},{19,11},{12,4},{20... | collective-permute-start | bytes 786440 | tf_op jit(solution)/shard_map/ppermute | solution.py:80
  284.5 9.5 %collective-permute-start.59 = (bf16[1024,128]{1,0:T(8,128)(2,1)S(1)}, bf16[1024,128]{1,0:T(8,128)(2,1)S(1)}, u32[]{:S(2)}, u32[]{:S(2)}) collective-permute-start(bf16[1024,128]{1,0:T(8,128)(2,1)S(1)} %get-tuple-element.419), channel_id=1, source_target_pairs={{8,0},{16,8},{9,1},{17,9},{10,2},{18,10},{11,3},{19,11},{12,4},{20... | collective-permute-start | bytes 786440 | tf_op jit(solution)/shard_map/ppermute | solution.py:80
  (64 other events, 683.9 us)
Sparse Core Ops, SparseCore 0:
  103.5 40.8 all-gather.4
  146.2 35.5 all-gather.6
